TPU v7x, 128 devices: a whole 4x4x4 slice. The times are simulated.
128 devices in a mesh: ty: 8 (over x, core), tx: 16 (over y, z).
Axes of the slice: x: 4, y: 4, z: 4, core: 2. Of those that a mesh axis runs over, the one named last changes fastest.
Arguments:
- amplitudes: bfloat16 [4096, 256, 256], P(('ty', 'tx')), may hold values from 0.099609375 to 4
- owners: int32 [4096, 1], P(('ty', 'tx')), may hold values from 0 to 15; in each aligned block of 32 rows (0 to 31, 32 to 63, ...) at most 3 rows name the same one
- offsets: int32 [4096, 2], P(('ty', 'tx')), may hold values from 0 to 511
- object_field: float32 [2, 4096, 8192], P(None, 'ty', 'tx'), may hold values from -6 to 6
- probe: float32 [2, 256, 256], replicated, may hold values from -6 to 6
Outputs:
- object_new: float32 [2, 4096, 8192], P(None, 'ty', 'tx')
- probe_step: float32 [2, 256, 256], replicated
Inputs may be any that keep to these rules, and one draw needn't show every extreme that they name: `owners`: among the patterns of one device no owner column is named more than 3 times, a bound that some block reaches.
All inputs are finite; a program needn't handle non-finite values.
Results may differ from a plain program's by a relative error of at most 0.0013.
The roundings to bfloat16 on the way count: a program that leaves them out, or rounds other values in their place, can miss the bound.
Values may be sent and summed in bfloat16 or wider, within the bound.
A program may use at most 320 MiB of HBM per device.

v0:
```python
import math

import jax
import jax.numpy as jnp
from jax import lax
from jax.sharding import PartitionSpec as P


def shifted(value, axis, steps):
    count = lax.axis_size(axis)
    initial, last = (max(0, -steps), min(count, count - steps))
    return lax.ppermute(value, axis, [(source, source + steps) for source in range(initial, last)])


def dft_tables(width, orient):
    steps_i = jnp.arange(width, dtype=jnp.int32)
    phase = steps_i[:, None] * steps_i[None, :] % width
    angles = phase.astype(jnp.float32) * (2.0 * math.pi / width)
    cos_table = (jnp.cos(angles) / math.sqrt(width)).astype(jnp.bfloat16)
    sin_table = (orient * jnp.sin(angles) / math.sqrt(width)).astype(jnp.bfloat16)
    col_table = jnp.concatenate(
        [jnp.concatenate([cos_table, -sin_table], 1), jnp.concatenate([sin_table, cos_table], 1)], 0
    )
    return (cos_table, sin_table, col_table)


def transform(field_in, tables):
    cos_table, sin_table, col_table = tables
    width = cos_table.shape[0]
    direct = jnp.einsum("pk,bkm->bpm", cos_table, field_in, preferred_element_type=jnp.float32)
    mixed = jnp.einsum("pk,bkm->bpm", sin_table, field_in, preferred_element_type=jnp.float32)
    real_part = direct[..., :width] + mixed[..., width:]
    imag_part = direct[..., width:] - mixed[..., :width]
    halfway = jnp.concatenate([real_part, imag_part], -1).astype(jnp.bfloat16)
    return jnp.einsum("bpk,km->bpm", halfway, col_table, preferred_element_type=jnp.float32)


def project(windows, amp_rows, live_mask, probe, forward, inverse):
    width = probe.shape[1]
    probe_re, probe_im = (probe[0], probe[1])
    obj_re, obj_im = (windows[:, 0], windows[:, 1])
    psi_re = probe_re * obj_re - probe_im * obj_im
    psi_im = probe_re * obj_im + probe_im * obj_re
    psi_b = jnp.concatenate([psi_re, psi_im], -1).astype(jnp.bfloat16)
    spectrum = transform(psi_b, forward)
    spec_re, spec_im = (spectrum[..., :width], spectrum[..., width:])
    ratio_mag = amp_rows.astype(jnp.float32) / jnp.sqrt(
        spec_re * spec_re + spec_im * spec_im + 0.01
    )
    projected = jnp.concatenate([spec_re * ratio_mag, spec_im * ratio_mag], -1).astype(jnp.bfloat16)
    revised = transform(projected, inverse)
    live_col = live_mask[:, None, None]
    diff_re = (revised[..., :width] - psi_re) * live_col
    diff_im = (revised[..., width:] - psi_im) * live_col
    obj_terms = jnp.stack(
        [
            probe_re * diff_re + probe_im * diff_im,
            probe_re * diff_im - probe_im * diff_re,
            (probe_re * probe_re + probe_im * probe_im) * live_col,
        ],
        1,
    )
    probe_terms = jnp.stack(
        [
            jnp.sum(obj_re * diff_re + obj_im * diff_im, 0),
            jnp.sum(obj_re * diff_im - obj_im * diff_re, 0),
            jnp.sum((obj_re * obj_re + obj_im * obj_im) * live_col, 0),
        ],
        0,
    )
    return (obj_terms, probe_terms)


def local(amplitudes, owners, offsets, object_field, probe):
    pattern_count = amplitudes.shape[0]
    width = amplitudes.shape[1]
    tile_side = object_field.shape[1]
    col_count = lax.axis_size("tx")
    row_count = lax.axis_size("ty")
    capacity = max(2, pattern_count // col_count + 1)
    slot_count = col_count * capacity
    row_index = lax.axis_index("ty")
    owner_col = owners[:, 0]
    local_row = jnp.minimum(offsets[:, 0], row_count * tile_side - width - row_index * tile_side)
    local_col = jnp.minimum(offsets[:, 1], col_count * tile_side - width - owner_col * tile_side)
    slot_ids = jnp.arange(slot_count, dtype=jnp.int32)
    positions = jnp.arange(pattern_count, dtype=jnp.int32)
    shared = (owner_col[:, None] == owner_col[None, :]) & (positions[:, None] > positions[None, :])
    target = owner_col * capacity + jnp.sum(shared.astype(jnp.int32), 1)
    select = target[None, :] == slot_ids[:, None]
    packed = jnp.dot(
        select.astype(jnp.bfloat16),
        amplitudes.reshape(pattern_count, width * width),
        preferred_element_type=jnp.float32,
    )
    packed = packed.astype(jnp.bfloat16).reshape(col_count, capacity, width, width)
    values = jnp.stack([local_row, local_col, jnp.ones_like(local_row)], 1)
    slot_info = jnp.sum(jnp.where(select[:, :, None], values[None, :, :], 0), 1).reshape(
        col_count, capacity, 3
    )
    got_amp, got_info = (
        lax.all_to_all(packed, "tx", split_axis=0, concat_axis=0, tiled=True),
        lax.all_to_all(slot_info, "tx", split_axis=0, concat_axis=0, tiled=True),
    )
    got_amp = got_amp.reshape(slot_count, width, width)
    got_info = got_info.reshape(slot_count, 3)
    right_strip = shifted(object_field[:, :, :width], "tx", -1)
    below_strip = shifted(object_field[:, :width, :], "ty", -1)
    corner_half = shifted(object_field[:, :width, :width], "tx", -1)
    corner_strip = shifted(corner_half, "ty", -1)
    upper = jnp.concatenate([object_field, right_strip], 2)
    lower = jnp.concatenate([below_strip, corner_strip], 2)
    extended = jnp.concatenate([upper, lower], 1)
    forward = dft_tables(width, 1.0)
    inverse = dft_tables(width, -1.0)
    block_rows = 8
    block_count = slot_count // block_rows
    live_all = got_info[:, 2].astype(jnp.float32)
    amp_blocks = got_amp.reshape(block_count, block_rows, width, width)
    row_blocks = got_info[:, 0].reshape(block_count, block_rows)
    col_blocks = got_info[:, 1].reshape(block_count, block_rows)
    live_blocks = live_all.reshape(block_count, block_rows)

    def advance(running, block_data):
        totals, probe_sums = running
        amp_rows, rows_here, cols_here, live_here = block_data
        windows = jax.vmap(
            lambda row_at, col_at: lax.dynamic_slice(
                extended, (jnp.int32(0), row_at, col_at), (2, width, width)
            )
        )(rows_here, cols_here)
        obj_terms, probe_terms = project(windows, amp_rows, live_here, probe, forward, inverse)

        def deposit(entry, totals_now):
            corner = (jnp.int32(0), rows_here[entry], cols_here[entry])
            current = lax.dynamic_slice(totals_now, corner, (3, width, width))
            return lax.dynamic_update_slice(totals_now, current + obj_terms[entry], corner)

        totals = lax.fori_loop(0, block_rows, deposit, totals)
        return ((totals, probe_sums + probe_terms), None)

    side = tile_side + width
    start_state = (
        jnp.zeros((3, side, side), jnp.float32),
        jnp.zeros((3, width, width), jnp.float32),
    )
    (totals, probe_sums), _ = lax.scan(
        advance, start_state, (amp_blocks, row_blocks, col_blocks, live_blocks)
    )
    right_in = shifted(totals[:, :tile_side, tile_side:], "tx", 1)
    below_in = shifted(totals[:, tile_side:, :tile_side], "ty", 1)
    corner_part = shifted(totals[:, tile_side:, tile_side:], "tx", 1)
    corner_in = shifted(corner_part, "ty", 1)
    summed = totals[:, :tile_side, :tile_side]
    summed = summed.at[:, :, :width].add(right_in)
    summed = summed.at[:, :width, :].add(below_in)
    summed = summed.at[:, :width, :width].add(corner_in)
    object_new = object_field + summed[:2] / (summed[2] + 1.0)
    total_num, total_den = lax.psum((probe_sums[:2], probe_sums[2]), ("ty", "tx"))
    probe_step = total_num / jnp.sqrt(total_den + 1.0)
    return (object_new, probe_step)


def solution(mesh):
    return jax.shard_map(
        local,
        mesh=mesh,
        in_specs=(
            P(("ty", "tx"), None, None),
            P(("ty", "tx"), None),
            P(("ty", "tx"), None),
            P(None, "ty", "tx"),
            P(),
        ),
        out_specs=(P(None, "ty", "tx"), P()),
        check_vma=False,
    )
```

profile of v0, /device:TPU:1, one launch (start us, length us, event | category | flops | bytes accessed | tf_op | source)
XLA Modules:
  0.0 1575.8 jit_solution(7969316345753638738)
XLA Ops:
  47.9 59.8 %collective-permute-done.2 = f32[2,256,256]{2,1,0:T(8,128)} collective-permute-done((f32[2,256,256]{2,1,0:T(8,128)S(1)}, f32[2,256,256]{2,1,0:T(8,128)}, u32[]{:S(2)}, u32[]{:S(2)}) %collective-permute-start.2) | collective-permute-done | bytes 524320 | tf_op jit(solution)/shard_map/ppermute | solution.py:12
  119.8 18.8 %collective-permute-done = f32[2,512,256]{2,1,0:T(8,128)} collective-permute-done((f32[2,512,256]{2,1,0:T(8,128)}, f32[2,512,256]{2,1,0:T(8,128)}, u32[]{:S(2)}, u32[]{:S(2)}) %collective-permute-start) | collective-permute-done | bytes 1048608 | tf_op jit(solution)/shard_map/ppermute | solution.py:12
  146.2 1203.2 %while.48 = (s32[]{:T(128)}, f32[3,768,768]{2,1,0:T(8,128)}, f32[3,256,256]{1,2,0:T(8,128)S(1)}, s32[6,8]{1,0:T(8,128)S(1)}, s32[6,8]{1,0:T(8,128)S(1)}, /*index...) while((s32[]{:T(128)}, f32[3,768,768]{2,1,0:T(8,128)}, ...), condition=%wide.region_8.9_spmd.clone.clone, body=%wide.region_2.8_spmd.clone.clone.sunk | while | flops 4357619712 | bytes 155715440 | solution.py:147
  146.2 35.2 %while.49 = (s32[]{:T(128)}, f32[2,768,768]{2,1,0:T(8,128)}, s32[8,3]{0,1:T(4,128)S(1)}, f32[8,2,256,256]{2,3,0,1:T(8,128)}, s32[]{:T(128)}) while((s32[]{:T(128)}, f32[2,768,768]{2,1,0:T(8,128)}, s32[8,3]{0,1:T(4,128)S(1)}, f32[8,2,256,256]{2,3,0,1:T(8,128)}, s32[]{:T(128)}) %tuple.147), condition=%wide.while_cond.3, body=%wide.while_body.3.sunk | while | flops 2 | bytes 3146353 | solution.py:128
  209.3 136.7 %while.50 = (s32[]{:T(128)}, f32[3,768,768]{2,1,0:T(8,128)}, s32[8]{0:T(128)S(1)}, s32[8]{0:T(128)S(1)}, f32[8,3,256,256]{2,3,0,1:T(8,128)}, /*index=5*/s32[]{:T(128)}, s32[]{:T(128)}, s32[]{:T(128)}) while((s32[]{:T(128)}, f32[3,768,768]{2,1,0:T(8,128)}, s32[8]{0:T(128)S(1)}, s32[8]{0:T(128)S(1)}, f32[8,3,256,256]{2,3,0,1:T(8,128)}, ...), condition=%wide.region_4.4_spmd, body=%wide.region_3.3_spmd.sunk | while | flops 196616 | bytes 7078081 | solution.py:139
  319.0 9.6 dynamic_update_slice.8
  346.0 35.2 %while.49 = (s32[]{:T(128)}, f32[2,768,768]{2,1,0:T(8,128)}, s32[8,3]{0,1:T(4,128)S(1)}, f32[8,2,256,256]{2,3,0,1:T(8,128)}, s32[]{:T(128)}) while((s32[]{:T(128)}, f32[2,768,768]{2,1,0:T(8,128)}, s32[8,3]{0,1:T(4,128)S(1)}, f32[8,2,256,256]{2,3,0,1:T(8,128)}, s32[]{:T(128)}) %tuple.147), condition=%wide.while_cond.3, body=%wide.while_body.3.sunk | while | flops 2 | bytes 3146353 | solution.py:128
  409.1 137.3 %while.50 = (s32[]{:T(128)}, f32[3,768,768]{2,1,0:T(8,128)}, s32[8]{0:T(128)S(1)}, s32[8]{0:T(128)S(1)}, f32[8,3,256,256]{2,3,0,1:T(8,128)}, /*index=5*/s32[]{:T(128)}, s32[]{:T(128)}, s32[]{:T(128)}) while((s32[]{:T(128)}, f32[3,768,768]{2,1,0:T(8,128)}, s32[8]{0:T(128)S(1)}, s32[8]{0:T(128)S(1)}, f32[8,3,256,256]{2,3,0,1:T(8,128)}, ...), condition=%wide.region_4.4_spmd, body=%wide.region_3.3_spmd.sunk | while | flops 196616 | bytes 7078081 | solution.py:139
  450.8 9.6 dynamic_update_slice.8
  485.0 9.6 dynamic_update_slice.8
  502.7 9.6 dynamic_update_slice.8
  536.9 9.6 dynamic_update_slice.8
  546.5 35.2 %while.49 = (s32[]{:T(128)}, f32[2,768,768]{2,1,0:T(8,128)}, s32[8,3]{0,1:T(4,128)S(1)}, f32[8,2,256,256]{2,3,0,1:T(8,128)}, s32[]{:T(128)}) while((s32[]{:T(128)}, f32[2,768,768]{2,1,0:T(8,128)}, s32[8,3]{0,1:T(4,128)S(1)}, f32[8,2,256,256]{2,3,0,1:T(8,128)}, s32[]{:T(128)}) %tuple.147), condition=%wide.while_cond.3, body=%wide.while_body.3.sunk | while | flops 2 | bytes 3146353 | solution.py:128
  609.6 137.4 %while.50 = (s32[]{:T(128)}, f32[3,768,768]{2,1,0:T(8,128)}, s32[8]{0:T(128)S(1)}, s32[8]{0:T(128)S(1)}, f32[8,3,256,256]{2,3,0,1:T(8,128)}, /*index=5*/s32[]{:T(128)}, s32[]{:T(128)}, s32[]{:T(128)}) while((s32[]{:T(128)}, f32[3,768,768]{2,1,0:T(8,128)}, s32[8]{0:T(128)S(1)}, s32[8]{0:T(128)S(1)}, f32[8,3,256,256]{2,3,0,1:T(8,128)}, ...), condition=%wide.region_4.4_spmd, body=%wide.region_3.3_spmd.sunk | while | flops 196616 | bytes 7078081 | solution.py:139
  617.8 9.6 dynamic_update_slice.8
  651.9 9.6 dynamic_update_slice.8
  720.9 9.6 dynamic_update_slice.8
  747.1 35.2 %while.49 = (s32[]{:T(128)}, f32[2,768,768]{2,1,0:T(8,128)}, s32[8,3]{0,1:T(4,128)S(1)}, f32[8,2,256,256]{2,3,0,1:T(8,128)}, s32[]{:T(128)}) while((s32[]{:T(128)}, f32[2,768,768]{2,1,0:T(8,128)}, s32[8,3]{0,1:T(4,128)S(1)}, f32[8,2,256,256]{2,3,0,1:T(8,128)}, s32[]{:T(128)}) %tuple.147), condition=%wide.while_cond.3, body=%wide.while_body.3.sunk | while | flops 2 | bytes 3146353 | solution.py:128
  810.2 138.5 %while.50 = (s32[]{:T(128)}, f32[3,768,768]{2,1,0:T(8,128)}, s32[8]{0:T(128)S(1)}, s32[8]{0:T(128)S(1)}, f32[8,3,256,256]{2,3,0,1:T(8,128)}, /*index=5*/s32[]{:T(128)}, s32[]{:T(128)}, s32[]{:T(128)}) while((s32[]{:T(128)}, f32[3,768,768]{2,1,0:T(8,128)}, s32[8]{0:T(128)S(1)}, s32[8]{0:T(128)S(1)}, f32[8,3,256,256]{2,3,0,1:T(8,128)}, ...), condition=%wide.region_4.4_spmd, body=%wide.region_3.3_spmd.sunk | while | flops 196616 | bytes 7078081 | solution.py:139
  818.3 9.6 dynamic_update_slice.8
  887.2 9.6 dynamic_update_slice.8
  939.1 9.6 dynamic_update_slice.8
  948.7 35.2 %while.49 = (s32[]{:T(128)}, f32[2,768,768]{2,1,0:T(8,128)}, s32[8,3]{0,1:T(4,128)S(1)}, f32[8,2,256,256]{2,3,0,1:T(8,128)}, s32[]{:T(128)}) while((s32[]{:T(128)}, f32[2,768,768]{2,1,0:T(8,128)}, s32[8,3]{0,1:T(4,128)S(1)}, f32[8,2,256,256]{2,3,0,1:T(8,128)}, s32[]{:T(128)}) %tuple.147), condition=%wide.while_cond.3, body=%wide.while_body.3.sunk | while | flops 2 | bytes 3146353 | solution.py:128
  1011.8 137.1 %while.50 = (s32[]{:T(128)}, f32[3,768,768]{2,1,0:T(8,128)}, s32[8]{0:T(128)S(1)}, s32[8]{0:T(128)S(1)}, f32[8,3,256,256]{2,3,0,1:T(8,128)}, /*index=5*/s32[]{:T(128)}, s32[]{:T(128)}, s32[]{:T(128)}) while((s32[]{:T(128)}, f32[3,768,768]{2,1,0:T(8,128)}, s32[8]{0:T(128)S(1)}, s32[8]{0:T(128)S(1)}, f32[8,3,256,256]{2,3,0,1:T(8,128)}, ...), condition=%wide.region_4.4_spmd, body=%wide.region_3.3_spmd.sunk | while | flops 196616 | bytes 7078081 | solution.py:139
  1088.0 9.6 dynamic_update_slice.8
  1149.0 35.2 %while.49 = (s32[]{:T(128)}, f32[2,768,768]{2,1,0:T(8,128)}, s32[8,3]{0,1:T(4,128)S(1)}, f32[8,2,256,256]{2,3,0,1:T(8,128)}, s32[]{:T(128)}) while((s32[]{:T(128)}, f32[2,768,768]{2,1,0:T(8,128)}, s32[8,3]{0,1:T(4,128)S(1)}, f32[8,2,256,256]{2,3,0,1:T(8,128)}, s32[]{:T(128)}) %tuple.147), condition=%wide.while_cond.3, body=%wide.while_body.3.sunk | while | flops 2 | bytes 3146353 | solution.py:128
  1212.1 137.3 %while.50 = (s32[]{:T(128)}, f32[3,768,768]{2,1,0:T(8,128)}, s32[8]{0:T(128)S(1)}, s32[8]{0:T(128)S(1)}, f32[8,3,256,256]{2,3,0,1:T(8,128)}, /*index=5*/s32[]{:T(128)}, s32[]{:T(128)}, s32[]{:T(128)}) while((s32[]{:T(128)}, f32[3,768,768]{2,1,0:T(8,128)}, s32[8]{0:T(128)S(1)}, s32[8]{0:T(128)S(1)}, f32[8,3,256,256]{2,3,0,1:T(8,128)}, ...), condition=%wide.region_4.4_spmd, body=%wide.region_3.3_spmd.sunk | while | flops 196616 | bytes 7078081 | solution.py:139
  1254.0 9.6 dynamic_update_slice.8
  1271.7 9.6 dynamic_update_slice.8
  1323.3 9.6 dynamic_update_slice.8
  1352.0 16.5 %collective-permute-start.4 = (f32[3,512,256]{2,1,0:T(8,128)}, f32[3,512,256]{2,1,0:T(8,128)}, u32[]{:S(2)}, u32[]{:S(2)}) collective-permute-start(f32[3,512,256]{2,1,0:T(8,128)} %slice.240), channel_id=1, source_target_pairs={{0,1},{1,2},{2,3},{3,4},{4,5},{5,6},{6,7},{7,8},{8,9},{9,10},{10,1... | collective-permute-start | bytes 4718600 | tf_op jit(solution)/shard_map/ppermute | solution.py:12
  1388.8 161.1 %all-reduce.3.cloned.1.call-done = (f32[2,256,256]{2,1,0:T(8,128)}, f32[256,256]{0,1:T(8,128)}) async-done(((f32[2,256,256]{2,1,0:T(8,128)}, f32[256,256]{0,1:T(8,128)}), (f32[2,256,256]{2,1,0:T(8,128)}, f32[256,256]{0,1:T(8,128)})) %all-reduce.3.cloned.1.call-update) | async-done | bytes 786448 | tf_op jit(solution)/shard_map/psum | solution.py:159
  (774 shorter events, 973.1 us)
Async XLA Ops:
  10.6 19.3 %all-to-all-start = ((s32[16,3,3]{1,2,0:T(4,128)}), s32[16,3,3]{1,2,0:T(4,128)S(1)}, u32[]{:S(2)}, u32[]{:S(2)}) async-start(s32[16,3,3]{1,2,0:T(4,128)} %copy.59), calls=%async_computation | async-start | bytes 65536 | tf_op jit(solution)/shard_map/all_to_all | solution.py:103
  29.8 6.9 copy-start.2
  29.8 112.9 %all-to-all-start.1 = ((bf16[16,3,256,256]{3,2,1,0:T(8,128)(2,1)}), bf16[16,3,256,256]{3,2,1,0:T(8,128)(2,1)}, u32[]{:S(2)}, u32[]{:S(2)}) async-start(bf16[16,3,256,256]{3,2,1,0:T(8,128)(2,1)} %bitcast.200), calls=%async_computation.1 | async-start | bytes 12582912 | tf_op jit(solution)/shard_map/all_to_all | solution.py:102
  36.7 1513.2 %all-reduce.3.cloned.1.call-start = ((), (), s32[]{:S(2)}) async-start(), calls=%async_computation.2 | async-start | bytes 1572864 | tf_op jit(solution)/shard_map/psum | solution.py:159
  36.8 71.0 %collective-permute-start.2 = (f32[2,256,256]{2,1,0:T(8,128)S(1)}, f32[2,256,256]{2,1,0:T(8,128)}, u32[]{:S(2)}, u32[]{:S(2)}) collective-permute-start(f32[2,256,256]{2,1,0:T(8,128)S(1)} %slice.234), channel_id=1, source_target_pairs={{1,0},{2,1},{3,2},{4,3},{5,4},{6,5},{7,6},{8,7},{9,8},{10,9},{11,1... | collective-permute-start | bytes 1572872 | tf_op jit(solution)/shard_map/ppermute | solution.py:12
  39.2 99.5 %collective-permute-start = (f32[2,512,256]{2,1,0:T(8,128)}, f32[2,512,256]{2,1,0:T(8,128)}, u32[]{:S(2)}, u32[]{:S(2)}) collective-permute-start(f32[2,512,256]{2,1,0:T(8,128)} %slice.232), channel_id=1, source_target_pairs={{1,0},{2,1},{3,2},{4,3},{5,4},{6,5},{7,6},{8,7},{9,8},{10,9},{11,1... | collective-permute-start | bytes 3145736 | tf_op jit(solution)/shard_map/ppermute | solution.py:12
  41.5 97.1 %collective-permute-start.1 = (f32[2,256,512]{2,1,0:T(8,128)}, f32[2,256,512]{2,1,0:T(8,128)}, u32[]{:S(2)}, u32[]{:S(2)}) collective-permute-start(f32[2,256,512]{2,1,0:T(8,128)} %slice.233), channel_id=1, source_target_pairs={{16,0},{32,16},{48,32},{64,48},{80,64},{96,80},{112,96},{17,1},{33... | collective-permute-start | bytes 3145736 | tf_op jit(solution)/shard_map/ppermute | solution.py:12
  107.7 30.9 %collective-permute-start.3 = (f32[2,256,256]{2,1,0:T(8,128)}, f32[2,256,256]{2,1,0:T(8,128)S(1)}, u32[]{:S(2)}, u32[]{:S(2)}) collective-permute-start(f32[2,256,256]{2,1,0:T(8,128)} %collective-permute-done.2), channel_id=1, source_target_pairs={{16,0},{32,16},{48,32},{64,48},{80,64},{96,80},{112,96},{17,1},{33... | collective-permute-start | bytes 1572872 | tf_op jit(solution)/shard_map/ppermute | solution.py:12
  188.6 1.0 copy-start.6
  196.2 1.0 copy-start.4
  197.2 2.2 copy-start
  203.0 1.8 copy-start.1
  388.4 1.0 copy-start.6
  396.0 1.0 copy-start.4
  397.1 2.2 copy-start
  402.9 1.8 copy-start.1
  588.9 1.0 copy-start.6
  596.5 1.0 copy-start.4
  597.6 2.2 copy-start
  603.4 1.8 copy-start.1
  789.4 1.0 copy-start.6
  798.1 2.2 copy-start
  803.9 1.8 copy-start.1
  999.8 2.2 copy-start
  1005.5 1.8 copy-start.1
  1200.0 2.2 copy-start
  1205.8 1.8 copy-start.1
  1352.0 206.0 %collective-permute-start.4 = (f32[3,512,256]{2,1,0:T(8,128)}, f32[3,512,256]{2,1,0:T(8,128)}, u32[]{:S(2)}, u32[]{:S(2)}) collective-permute-start(f32[3,512,256]{2,1,0:T(8,128)} %slice.240), channel_id=1, source_target_pairs={{0,1},{1,2},{2,3},{3,4},{4,5},{5,6},{6,7},{7,8},{8,9},{9,10},{10,1... | collective-permute-start | bytes 4718600 | tf_op jit(solution)/shard_map/ppermute | solution.py:12
  1371.2 189.0 %collective-permute-start.5 = (f32[3,256,512]{2,1,0:T(8,128)}, f32[3,256,512]{2,1,0:T(8,128)}, u32[]{:S(2)}, u32[]{:S(2)}) collective-permute-start(f32[3,256,512]{2,1,0:T(8,128)} %slice.242), channel_id=1, source_target_pairs={{0,16},{16,32},{32,48},{48,64},{64,80},{80,96},{96,112},{1,17},{17... | collective-permute-start | bytes 4718600 | tf_op jit(solution)/shard_map/ppermute | solution.py:12
  1381.1 171.6 %collective-permute-start.6 = (f32[3,256,256]{2,1,0:T(8,128)}, f32[3,256,256]{2,1,0:T(8,128)}, u32[]{:S(2)}, u32[]{:S(2)}) collective-permute-start(f32[3,256,256]{2,1,0:T(8,128)} %slice.244), channel_id=1, source_target_pairs={{0,1},{1,2},{2,3},{3,4},{4,5},{5,6},{6,7},{7,8},{8,9},{9,10},{10,1... | collective-permute-start | bytes 2359304 | tf_op jit(solution)/shard_map/ppermute | solution.py:12
  1552.7 12.7 collective-permute-start.7
  1565.4 1.6 copy-start.3
  (11 other events, 10.9 us)
Sparse Core Ops, SparseCore 0:
  1386.7 163.1 all-reduce.2
where the time goes:
time: 1600 us; the launch traced here: 1580 us
  local copies, waits for them, and re-layouts  819 us (51%)
  waiting for transfers between devices  243 us (15%)
  other arithmetic  194 us (12%)
  loops' own time  189 us (12%)
  starting transfers between devices  59.5 us (4%)
  matrix products  57.6 us (4%)
    dynamic_update_slice x48, local copies, waits for them, and re-layouts, deposit(): lax.dynamic_update_slice(totals_now, current + obj_terms[entry], corner)  434 us
    gather x240, local copies, waits for them, and re-layouts  211 us
    another operation x6, loops' own time, advance(): totals = lax.fori_loop(0, block_rows, deposit, totals)  187 us
    psum x1, waiting for transfers between devices, local(): lax.psum((probe_sums[:2], probe_sums[2]), ('ty', 'tx'))  161 us
    ppermute x8, waiting for transfers between devices, shifted(): lax.ppermute(value, axis, [(source, source + steps) for source in range(i...  81.7 us
    add x48, other arithmetic, deposit(): current + obj_terms[entry]  76.3 us
    dynamic_slice x96, local copies, waits for them, and re-layouts, deposit(): obj_terms[entry]  70 us
    dynamic_slice x96, local copies, waits for them, and re-layouts, deposit(): corner = (jnp.int32(0), rows_here[entry], cols_here[entry])  56.2 us
  transfers between devices with their start and end apart: 11, of which 4 were waited for; matrix products, arithmetic and copies ran while one was open for 3% of the time, Pallas kernels for 0%

commit v1 on v0

v1 whole, which is shorter than its diff:
```python
import functools
import math

import jax
import jax.numpy as jnp
from jax import lax
from jax.experimental import pallas as pl
from jax.experimental.pallas import tpu as pltpu
from jax.sharding import PartitionSpec as P

W = 256
T = 512
SIDE = T + W
CAP = 3
RB = 32
LB = 128
MIB = 2**20


def shifted(value, axis, steps):
    count = lax.axis_size(axis)
    initial, last = (max(0, -steps), min(count, count - steps))
    return lax.ppermute(value, axis, [(source, source + steps) for source in range(initial, last)])


def tables():
    steps = jnp.arange(W, dtype=jnp.int32)
    phase = steps[:, None] * steps[None, :] % W
    angles = phase.astype(jnp.float32) * (2.0 * math.pi / W)
    c = (jnp.cos(angles) / math.sqrt(W)).astype(jnp.bfloat16)
    s = (jnp.sin(angles) / math.sqrt(W)).astype(jnp.bfloat16)
    ta = jnp.concatenate([jnp.concatenate([c, s], 1), jnp.concatenate([-s, c], 1)], 0)
    tb = jnp.concatenate([jnp.concatenate([c, -s], 1), jnp.concatenate([s, c], 1)], 0)
    return ta, tb


def pack_kernel(cols, owners, offsets, amp, packed, info, count, sem):
    n = amp.shape[0]
    rows_end = (lax.axis_size("ty") * T - W) - lax.axis_index("ty") * T
    for o in range(cols):
        count[o] = 0
        for k in range(4 * CAP):
            info[o, k] = 0

    def place(i, carry):
        o = owners[i, 0]
        k = count[o]
        count[o] = k + 1
        info[o, 4 * k] = jnp.minimum(offsets[i, 0], rows_end)
        info[o, 4 * k + 1] = jnp.minimum(offsets[i, 1], cols * T - W - o * T)
        info[o, 4 * k + 2] = 1
        pltpu.make_async_copy(amp.at[i], packed.at[k, o], sem.at[i]).start()
        return carry

    lax.fori_loop(0, n, place, 0)

    def finish(i, carry):
        pltpu.make_async_copy(amp.at[0], packed.at[0, 0], sem.at[i]).wait()
        return carry

    lax.fori_loop(0, n, finish, 0)


def pack(amp, owners, offsets):
    cols = lax.axis_size("tx")
    n = amp.shape[0]
    smem = pl.BlockSpec(memory_space=pltpu.SMEM)
    hbm = pl.BlockSpec(memory_space=pl.ANY)
    return pl.pallas_call(
        functools.partial(pack_kernel, cols),
        out_shape=(
            jax.ShapeDtypeStruct((CAP, cols, W, W), amp.dtype),
            jax.ShapeDtypeStruct((cols, 4 * CAP), jnp.int32),
        ),
        in_specs=[smem, smem, pl.BlockSpec(memory_space=pltpu.VMEM)],
        out_specs=(hbm, smem),
        scratch_shapes=[pltpu.SMEM((cols,), jnp.int32), pltpu.SemaphoreType.DMA((n,))],
        name="pack",
    )(owners, offsets, amp)


def chunk_kernel(slot, first, info, amp, obj, right, below, corner, probe, ta, tb, acc_in, ps_in, acc, ps, ext, win, xs, ys, sem):
    n = amp.shape[0]
    copies = []
    for p in range(2):
        for b in range(4):
            lanes = pl.ds(b * LB, LB)
            copies.append((obj.at[p, :, lanes], ext.at[p, b, pl.ds(0, T), :]))
            copies.append((below.at[p, :, lanes], ext.at[p, b, pl.ds(T, W), :]))
        for b in range(2):
            lanes = pl.ds(b * LB, LB)
            copies.append((right.at[p, :, lanes], ext.at[p, 4 + b, pl.ds(0, T), :]))
            copies.append((corner.at[p, :, lanes], ext.at[p, 4 + b, pl.ds(T, W), :]))
    if not first:
        copies.append((acc_in, acc))
        copies.append((ps_in, ps))
    copies = [pltpu.make_async_copy(a, b, sem.at[i]) for i, (a, b) in enumerate(copies)]
    for copy in copies:
        copy.start()
    if first:
        def clear(i, carry):
            for p in range(2):
                for b in range(6):
                    acc[p, b, pl.ds(i * RB, RB), :] = jnp.zeros((RB, LB), jnp.float32)
            return carry

        lax.fori_loop(0, SIDE // RB, clear, 0)
        ps[...] = jnp.zeros(ps.shape, jnp.float32)
    for copy in copies:
        copy.wait()
    lane = lax.broadcasted_iota(jnp.int32, (RB, LB), 1)

    def body(i, carry):
        r = info[i, 4 * slot]
        c = info[i, 4 * slot + 1]

        @pl.when(info[i, 4 * slot + 2] > 0)
        def _():
            cb = c // LB
            cs = c % LB
            back = (LB - cs) % LB
            low = lane < LB - cs
            high = lane >= cs
            for k in range(0, W, RB):
                o = []
                for p in range(2):
                    b = [pltpu.roll(ext[p, cb + j, pl.ds(r + k, RB), :], back, 1) for j in range(3)]
                    o.append([jnp.where(low, b[0], b[1]), jnp.where(low, b[1], b[2])])
                for h in range(2):
                    sl = slice(h * LB, h * LB + LB)
                    ore, oim = o[0][h], o[1][h]
                    win[0, k:k + RB, sl] = ore
                    win[1, k:k + RB, sl] = oim
                    pr, pi = probe[0, k:k + RB, sl], probe[1, k:k + RB, sl]
                    xs[k:k + RB, sl] = (pr * ore - pi * oim).astype(jnp.bfloat16)
                    xs[W + k:W + k + RB, sl] = (pr * oim + pi * ore).astype(jnp.bfloat16)
            y = jnp.dot(ta[...], xs[...], preferred_element_type=jnp.float32).astype(jnp.bfloat16)
            ys[:, :W] = y[:W]
            ys[:, W:] = y[W:]
            z = jnp.dot(ys[...], tb[...], preferred_element_type=jnp.float32)
            zr, zi = z[:, :W], z[:, W:]
            q = amp[i].astype(jnp.float32) * lax.rsqrt(zr * zr + zi * zi + 0.01)
            xs[:W] = (zr * q).astype(jnp.bfloat16)
            xs[W:] = (zi * q).astype(jnp.bfloat16)
            y = jnp.dot(tb[...], xs[...], preferred_element_type=jnp.float32).astype(jnp.bfloat16)
            ys[:, :W] = y[:W]
            ys[:, W:] = y[W:]
            z = jnp.dot(ys[...], ta[...], preferred_element_type=jnp.float32)
            for k in range(0, W, RB):
                t = [[], []]
                for h in range(2):
                    sl = slice(h * LB, h * LB + LB)
                    ore, oim = win[0, k:k + RB, sl], win[1, k:k + RB, sl]
                    pr, pi = probe[0, k:k + RB, sl], probe[1, k:k + RB, sl]
                    dr = z[k:k + RB, sl] - (pr * ore - pi * oim)
                    di = z[k:k + RB, W + h * LB:W + h * LB + LB] - (pr * oim + pi * ore)
                    t[0].append(pr * dr + pi * di)
                    t[1].append(pr * di - pi * dr)
                    ps[0, k:k + RB, sl] += ore * dr + oim * di
                    ps[1, k:k + RB, sl] += ore * di - oim * dr
                    ps[2, k:k + RB, sl] += ore * ore + oim * oim
                for p in range(2):
                    a = [pltpu.roll(t[p][h], cs, 1) for h in range(2)]
                    out = [jnp.where(high, a[0], 0.0), jnp.where(high, a[1], a[0]), jnp.where(high, 0.0, a[1])]
                    for j in range(3):
                        acc[p, cb + j, pl.ds(r + k, RB), :] += out[j]
        return carry

    lax.fori_loop(0, n, body, 0)


def chunk(slot, info, amp, obj, right, below, corner, probe, ta, tb, acc, ps):
    first = acc is None
    vm = pl.BlockSpec(memory_space=pltpu.VMEM)
    hbm = pl.BlockSpec(memory_space=pl.ANY)
    acc_shape = (2, SIDE // LB, SIDE, LB)
    ps_shape = (3, W, W)
    if first:
        acc = jnp.zeros((8, LB), jnp.float32)
        ps = acc
    return pl.pallas_call(
        functools.partial(chunk_kernel, slot, first),
        out_shape=(jax.ShapeDtypeStruct(acc_shape, jnp.float32), jax.ShapeDtypeStruct(ps_shape, jnp.float32)),
        in_specs=[pl.BlockSpec(memory_space=pltpu.SMEM), vm, hbm, hbm, hbm, hbm, vm, vm, vm, hbm, hbm],
        out_specs=(vm, vm),
        scratch_shapes=[
            pltpu.VMEM((2, SIDE // LB, SIDE, LB), jnp.float32),
            pltpu.VMEM((2, W, W), jnp.float32),
            pltpu.VMEM((2 * W, W), jnp.bfloat16),
            pltpu.VMEM((W, 2 * W), jnp.bfloat16),
            pltpu.SemaphoreType.DMA((26,)),
        ],
        compiler_params=pltpu.CompilerParams(vmem_limit_bytes=50 * MIB),
        cost_estimate=pl.CostEstimate(flops=16 * 540_000_000, bytes_accessed=40_000_000, transcendentals=16 * W * W),
        name="project_slot",
    )(info, amp, obj, right, below, corner, probe, ta, tb, acc, ps)


def den_kernel(info, probe, den, pp):
    def clear(i, carry):
        for b in range(SIDE // LB):
            den[b, pl.ds(i * RB, RB), :] = jnp.zeros((RB, LB), jnp.float32)
        return carry

    lax.fori_loop(0, SIDE // RB, clear, 0)
    for h in range(2):
        lanes = slice(h * LB, h * LB + LB)
        pp[h] = probe[0, :, lanes] * probe[0, :, lanes] + probe[1, :, lanes] * probe[1, :, lanes]
    lane = lax.broadcasted_iota(jnp.int32, (RB, LB), 1)

    for slot in range(CAP):
        def body(i, carry):
            r = info[i, 4 * slot]
            c = info[i, 4 * slot + 1]

            @pl.when(info[i, 4 * slot + 2] > 0)
            def _():
                cb = c // LB
                cs = c % LB
                high = lane >= cs
                for k in range(0, W, RB):
                    a = [pltpu.roll(pp[h, k:k + RB, :], cs, 1) for h in range(2)]
                    out = [jnp.where(high, a[0], 0.0), jnp.where(high, a[1], a[0]), jnp.where(high, 0.0, a[1])]
                    for j in range(3):
                        den[cb + j, pl.ds(r + k, RB), :] += out[j]

            return carry

        lax.fori_loop(0, info.shape[0], body, 0)


def denominator(info, probe):
    vm = pl.BlockSpec(memory_space=pltpu.VMEM)
    return pl.pallas_call(
        den_kernel,
        out_shape=jax.ShapeDtypeStruct((SIDE // LB, SIDE, LB), jnp.float32),
        in_specs=[pl.BlockSpec(memory_space=pltpu.SMEM), vm],
        out_specs=vm,
        scratch_shapes=[pltpu.VMEM((2, W, LB), jnp.float32)],
        compiler_params=pltpu.CompilerParams(vmem_limit_bytes=16 * MIB),
        cost_estimate=pl.CostEstimate(flops=40_000_000, bytes_accessed=3_000_000, transcendentals=0),
        name="denominator",
    )(info, probe)


def tail_kernel(
    acc, ps, den, den_right, den_below, den_corner, obj, out, step,
    s_right, s_below, s_corner, g_right, g_below, g_corner, inv, ra, sb, rb, gc, gd,
    sa, qa, sbs, qb, scs, qc, sds, qd, ses, qe,
):
    ny, nx = lax.axis_size("ty"), lax.axis_size("tx")
    ty, tx = lax.axis_index("ty"), lax.axis_index("tx")
    barrier = pltpu.get_barrier_semaphore()
    down, up = lax.rem(ty + 1, ny), lax.rem(ty + ny - 1, ny)
    east, west = lax.rem(tx + 1, nx), lax.rem(tx + nx - 1, nx)
    greet = [(lax.rem(ty + d, ny), tx) for d in range(1, ny)] + [(ty, lax.rem(tx + d, nx)) for d in range(1, nx)]
    greet += [(down, east), (up, west)]
    for other in greet:
        pl.semaphore_signal(barrier, inc=1, device_id=other, device_id_type=pl.DeviceIdType.MESH)

    for p in range(2):
        for b in range(2):
            s_right[p, b] = acc[p, 4 + b, :T, :].astype(jnp.bfloat16)
            s_corner[p, b] = acc[p, 4 + b, T:, :].astype(jnp.bfloat16)
        for b in range(4):
            s_below[p, b] = acc[p, b, T:, :].astype(jnp.bfloat16)
    pl.semaphore_wait(barrier, len(greet))

    def send(src, dst, s, q, device):
        copy = pltpu.make_async_remote_copy(
            src_ref=src, dst_ref=dst, send_sem=s, recv_sem=q, device_id=device, device_id_type=pl.DeviceIdType.MESH
        )
        copy.start()
        return copy

    rows = W // ny
    stage_a = []
    for d in range(1, ny):
        peer = lax.rem(ty + d, ny)
        stage_a.append(
            send(ps.at[:, pl.ds(pl.multiple_of(peer * rows, rows), rows), :], ra.at[ty], sa.at[d - 1], qa.at[d - 1], (peer, tx))
        )
    strips = [
        send(s_right, g_right, ses.at[0], qe.at[0], (ty, east)),
        send(s_corner, g_corner, ses.at[1], qe.at[1], (down, east)),
        send(s_below, g_below, ses.at[2], qe.at[2], (down, tx)),
    ]
    ra[ty] = ps[:, pl.ds(pl.multiple_of(ty * rows, rows), rows), :]

    for b in range(4):
        total = den[b, :T, :]
        if b < 2:
            total = total + den_right[b]
        low = den_below[b]
        if b < 2:
            low = low + den_corner[b]
        inv[b, :W, :] = 1.0 / (total[:W] + low + 1.0)
        inv[b, W:, :] = 1.0 / (total[W:] + 1.0)

    for copy in stage_a:
        copy.wait_recv()
    total = ra[0]
    for j in range(1, ny):
        total = total + ra[j]
    for j in range(nx):
        p, g, h = j // (nx // 2), j // 2 % (rows // 8), j % 2
        lanes = slice(h * LB, h * LB + LB)
        sb[j, 0] = total[p, g * 8:g * 8 + 8, lanes]
        sb[j, 1] = total[2, g * 8:g * 8 + 8, lanes]
    stage_b = []
    for d in range(1, nx):
        peer = lax.rem(tx + d, nx)
        stage_b.append(send(sb.at[peer], rb.at[tx], sbs.at[d - 1], qb.at[d - 1], (ty, peer)))
    rb[tx] = sb[tx]
    for copy in stage_b:
        copy.wait_recv()
    total = rb[0]
    for j in range(1, nx):
        total = total + rb[j]
    gc[tx] = total[0] / jnp.sqrt(total[1] + 1.0)
    stage_c = []
    for d in range(1, nx):
        peer = lax.rem(tx + d, nx)
        stage_c.append(send(gc.at[tx], gc.at[tx], scs.at[d - 1], qc.at[d - 1], (ty, peer)))
    for copy in stage_c:
        copy.wait_recv()
    gd[ty] = gc[...]
    stage_d = []
    for d in range(1, ny):
        peer = lax.rem(ty + d, ny)
        stage_d.append(send(gc, gd.at[ty], sds.at[d - 1], qd.at[d - 1], (peer, tx)))

    for copy in strips:
        copy.wait_recv()
    has_west = jnp.where(tx > 0, 1.0, 0.0)
    has_north = jnp.where(ty > 0, 1.0, 0.0)
    has_both = has_west * has_north

    def upper(i, carry):
        at = pl.ds(pl.multiple_of(i * RB, RB), RB)
        for b in range(4):
            lanes = slice(b * LB, b * LB + LB)
            for p in range(2):
                num = acc[p, b, at, :] + has_north * g_below[p, b, at, :].astype(jnp.float32)
                if b < 2:
                    num = num + has_west * g_right[p, b, at, :].astype(jnp.float32)
                    num = num + has_both * g_corner[p, b, at, :].astype(jnp.float32)
                out[p, at, lanes] = obj[p, at, lanes] + num * inv[b, at, :]
        return carry

    def lower(i, carry):
        at = pl.ds(pl.multiple_of(i * RB, RB), RB)
        for b in range(4):
            lanes = slice(b * LB, b * LB + LB)
            for p in range(2):
                num = acc[p, b, at, :]
                if b < 2:
                    num = num + has_west * g_right[p, b, at, :].astype(jnp.float32)
                out[p, at, lanes] = obj[p, at, lanes] + num * inv[b, at, :]
        return carry

    lax.fori_loop(0, W // RB, upper, 0)
    lax.fori_loop(W // RB, T // RB, lower, 0)

    for copy in stage_d:
        copy.wait_recv()
    for t in range(ny):
        for j in range(nx):
            p, g, h = j // (nx // 2), j // 2 % (rows // 8), j % 2
            step[p, t * rows + g * 8:t * rows + g * 8 + 8, h * LB:h * LB + LB] = gd[t, j]
    for copy in stage_a + strips + stage_b + stage_c + stage_d:
        copy.wait_send()


def tail(acc, ps, den, den_right, den_below, den_corner, obj):
    ny, nx = lax.axis_size("ty"), lax.axis_size("tx")
    vm = pl.BlockSpec(memory_space=pltpu.VMEM)
    bf, f32 = jnp.bfloat16, jnp.float32
    dma = pltpu.SemaphoreType.DMA
    strips = [(2, 2, T, LB), (2, 4, W, LB), (2, 2, W, LB)]
    return pl.pallas_call(
        tail_kernel,
        out_shape=(jax.ShapeDtypeStruct(obj.shape, f32), jax.ShapeDtypeStruct((2, W, W), f32)),
        in_specs=[vm] * 7,
        out_specs=(vm, vm),
        scratch_shapes=[pltpu.VMEM(x, bf) for x in strips + strips]
        + [
            pltpu.VMEM((4, T, LB), f32),
            pltpu.VMEM((ny, 3, W // ny, W), f32),
            pltpu.VMEM((nx, 2, 8, LB), f32),
            pltpu.VMEM((nx, 2, 8, LB), f32),
            pltpu.VMEM((nx, 8, LB), f32),
            pltpu.VMEM((ny, nx, 8, LB), f32),
        ]
        + [dma((k,)) for k in (ny - 1, ny - 1, nx - 1, nx - 1, nx - 1, nx - 1, ny - 1, ny - 1, 3, 3)],
        compiler_params=pltpu.CompilerParams(vmem_limit_bytes=50 * MIB, collective_id=0, has_side_effects=True),
        name="exchange",
    )(acc, ps, den, den_right, den_below, den_corner, obj)


def local(amplitudes, owners, offsets, object_field, probe):
    right = shifted(object_field[:, :, :W], "tx", -1)
    below = shifted(object_field[:, :W, :], "ty", -1)
    corner = shifted(right[:, :W, :], "ty", -1)
    packed, info = pack(amplitudes, owners, offsets)
    got_info = lax.all_to_all(info, "tx", split_axis=0, concat_axis=0, tiled=True)
    den = denominator(got_info, probe)
    den_right = shifted(den[4:, :T], "tx", 1)
    den_below = shifted(den[:, T:], "ty", 1)
    den_corner = shifted(den_below[4:], "tx", 1)
    ta, tb = tables()
    acc, ps = None, None
    for slot in range(CAP):
        got = lax.all_to_all(packed[slot], "tx", split_axis=0, concat_axis=0, tiled=True)
        acc, ps = chunk(slot, got_info, got, object_field, right, below, corner, probe, ta, tb, acc, ps)
    return tail(acc, ps, den, den_right, den_below, den_corner, object_field)


def solution(mesh):
    return jax.shard_map(
        local,
        mesh=mesh,
        in_specs=(
            P(("ty", "tx"), None, None),
            P(("ty", "tx"), None),
            P(("ty", "tx"), None),
            P(None, "ty", "tx"),
            P(),
        ),
        out_specs=(P(None, "ty", "tx"), P()),
        check_vma=False,
    )
```

time: 1600 us -> 301 us (0.19); the launches traced: 1580 us -> 300 us
  local copies, waits for them, and re-layouts: 819 us -> 19.1 us
  waiting for transfers between devices: 243 us -> 27.5 us
  other arithmetic: 194 us -> 2.17 us
  loops' own time: 189 us -> 0 us
  Pallas kernels: 0 us -> 175 us
  matrix products: 57.6 us -> 0 us
  blocking collectives: 0 us -> 31.4 us
    dynamic_update_slice x48 -> x0, local copies, waits for them, and re-layouts: 434 us -> none  [deposit(): lax.dynamic_update_slice(totals_now, current + obj_terms[entry], corner)]
    gather x240 -> x0, local copies, waits for them, and re-layouts: 211 us -> none
    another operation x13 -> x0, loops' own time: 189 us -> none  [the longest x6 187 us: advance(): totals = lax.fori_loop(0, block_rows, deposit, totals)]
    pallas_call x0 -> x6, Pallas kernels: none -> 175 us  [the longest x3 87 us: chunk(): pl.pallas_call(functools.partial(chunk_kernel, slot, first), out_shape=(j...]
    psum x1 -> x0, waiting for transfers between devices: 161 us -> none  [local(): lax.psum((probe_sums[:2], probe_sums[2]), ('ty', 'tx'))]
    dynamic_slice x192 -> x0, local copies, waits for them, and re-layouts: 126 us -> none  [the longest x96 70 us: deposit(): obj_terms[entry]]
    add x57 -> x0, other arithmetic: 89.6 us -> none  [the longest x48 76.3 us: deposit(): current + obj_terms[entry]]
    another operation x37 -> x0, other arithmetic: 63.1 us -> none
  transfers between devices with their start and end apart: 11 -> 9, of which waited for: 4 -> 2; matrix products, arithmetic and copies ran while one was open for 3% -> 4% of each run, Pallas kernels for 0% -> 31%
where the time goes in v1:
time: 301 us; the launch traced here: 300 us
  Pallas kernels  175 us (58%)
  starting transfers between devices  43.7 us (15%)
  blocking collectives  31.4 us (10%)
  waiting for transfers between devices  27.5 us (9%)
  local copies, waits for them, and re-layouts  19.1 us (6%)
    pallas_call x3, Pallas kernels, chunk(): pl.pallas_call(functools.partial(chunk_kernel, slot, first), out_shape=(j...  87 us
    pallas_call x1, Pallas kernels, tail(): pl.pallas_call(tail_kernel, out_shape=(jax.ShapeDtypeStruct(obj.shape, f3...  77.4 us
    all_to_all x1, blocking collectives, local(): lax.all_to_all(packed[slot], 'tx', split_axis=0, concat_axis=0, tiled=True)  31.4 us
    ppermute x6, waiting for transfers between devices, shifted(): lax.ppermute(value, axis, [(source, source + steps) for source in range(i...  26.6 us
    ppermute x6, starting transfers between devices, shifted(): lax.ppermute(value, axis, [(source, source + steps) for source in range(i...  21.7 us
    all_to_all x2, starting transfers between devices, local(): lax.all_to_all(packed[slot], 'tx', split_axis=0, concat_axis=0, tiled=True)  13.4 us
    unnamed x26, local copies, waits for them, and re-layouts  9.67 us
    all_to_all x1, starting transfers between devices, local(): lax.all_to_all(info, 'tx', split_axis=0, concat_axis=0, tiled=True)  8.62 us
  transfers between devices with their start and end apart: 9, of which 2 were waited for; matrix products, arithmetic and copies ran while one was open for 4% of the time, Pallas kernels for 31%

profile of v1, /device:TPU:1, one launch (start us, length us, event | category | flops | bytes accessed | tf_op | source)
XLA Modules:
  0.0 300.2 jit_solution(18435730273073674637)
XLA Ops:
  0.6 1.3 copy.9.owners
  2.0 1.4 copy.10.offsets
  3.3 5.2 %pack.1 = (bf16[3,16,256,256]{3,2,1,0:T(8,128)(2,1)}, s32[16,12]{1,0:T(8,128)}) custom-call(s32[32,1]{1,0:T(8,128)} %copy.9.owners, s32[32,2]{1,0:T(8,128)} %copy.10.offsets, bf16[32,256,256]{2,1,0:T(8,128)(2,1)} %amp.1), custom_call_target="tpu_custom_call" | custom-call | tf_op jit(solution)/shard_map/pack/pallas_call | solution.py:69
  8.6 8.6 %all-to-all-start = ((s32[16,1,12]{2,1,0:T(1,128)}), s32[16,1,12]{2,1,0:T(1,128)S(1)}, u32[]{:S(2)}, u32[]{:S(2)}) async-start(s32[16,1,12]{2,1,0:T(1,128)} %bitcast.14), calls=%async_computation | async-start | bytes 16384 | tf_op jit(solution)/shard_map/all_to_all | solution.py:406
  17.2 5.5 %slice_bitcast_fusion = (bf16[16,256,256]{2,1,0:T(8,128)(2,1)}, bf16[16,256,256]{2,1,0:T(8,128)(2,1)S(1)}, bf16[16,256,256]{2,1,0:T(8,128)(2,1)}) fusion(bf16[3,16,256,256]{3,2,1,0:T(8,128)(2,1)} %get-tuple-element.11), kind=kLoop, calls=%fused_computation | loop fusion | bytes 12582912 | tf_op jit(solution)/shard_map/squeeze | solution.py:414
  22.7 0.9 all-to-all-done
  23.6 31.4 %all_to_all.26.amp = bf16[16,256,256]{2,1,0:T(8,128)(2,1)} all-to-all(bf16[16,256,256]{2,1,0:T(8,128)(2,1)S(1)} %get-tuple-element.19), channel_id=1, replica_groups=mesh['ty'=8,'tx'=16] {'tx'}, dimensions={0} | all-to-all | bytes 4194304 | tf_op jit(solution)/shard_map/all_to_all | solution.py:414
  55.0 4.9 %all-to-all-start.3 = ((bf16[16,256,256]{2,1,0:T(8,128)(2,1)}), bf16[16,256,256]{2,1,0:T(8,128)(2,1)}, u32[]{:S(2)}, u32[]{:S(2)}) async-start(bf16[16,256,256]{2,1,0:T(8,128)(2,1)} %get-tuple-element.18), calls=%async_computation.3 | async-start | bytes 4194304 | tf_op jit(solution)/shard_map/all_to_all | solution.py:414
  60.1 1.4 collective-permute-start
  61.5 1.0 slice.29
  62.6 5.1 %collective-permute-start.1 = (f32[2,256,512]{2,1,0:T(8,128)}, f32[2,256,512]{2,1,0:T(8,128)}, u32[]{:S(2)}, u32[]{:S(2)}) collective-permute-start(f32[2,256,512]{2,1,0:T(8,128)} %slice.29), channel_id=1, source_target_pairs={{16,0},{32,16},{48,32},{64,48},{80,64},{96,80},{112,96},{17,1},{33... | collective-permute-start | bytes 3145736 | tf_op jit(solution)/shard_map/ppermute | solution.py:23
  67.7 5.8 %denominator.1.den = f32[6,768,128]{2,1,0:T(8,128)S(1)} custom-call(s32[16,12]{1,0:T(8,128)S(1)} %bitcast.10, f32[2,256,256]{2,1,0:T(8,128)S(1)} %copy-done.1), custom_call_target="tpu_custom_call" | custom-call | flops 40000000 | bytes 3000000 | tf_op jit(solution)/shard_map/denominator/pallas_call | solution.py:234
  73.5 1.0 slice.38
  74.5 3.0 collective-permute-start.4
  77.5 26.6 %collective-permute-done.right = f32[2,512,256]{2,1,0:T(8,128)S(1)} collective-permute-done((f32[2,512,256]{2,1,0:T(8,128)S(1)}, f32[2,512,256]{2,1,0:T(8,128)S(1)}, u32[]{:S(2)}, u32[]{:S(2)}) %collective-permute-start) | collective-permute-done | bytes 1048608 | tf_op jit(solution)/shard_map/ppermute | solution.py:23
  104.1 0.8 slice.36
  104.9 1.0 copy-done.8
  105.9 5.9 %collective-permute-start.2 = (f32[2,256,256]{2,1,0:T(8,128)}, f32[2,256,256]{2,1,0:T(8,128)}, u32[]{:S(2)}, u32[]{:S(2)}) collective-permute-start(f32[2,256,256]{2,1,0:T(8,128)} %slice.36), channel_id=1, source_target_pairs={{16,0},{32,16},{48,32},{64,48},{80,64},{96,80},{112,96},{17,1},{33... | collective-permute-start | bytes 1572872 | tf_op jit(solution)/shard_map/ppermute | solution.py:23
  111.8 8.4 %all-to-all-start.1 = ((bf16[16,256,256]{2,1,0:T(8,128)(2,1)}), bf16[16,256,256]{2,1,0:T(8,128)(2,1)}, u32[]{:S(2)}, u32[]{:S(2)}) async-start(bf16[16,256,256]{2,1,0:T(8,128)(2,1)} %get-tuple-element.20), calls=%async_computation.1 | async-start | bytes 4194304 | tf_op jit(solution)/shard_map/all_to_all | solution.py:414
  120.3 1.0 fusion.8
  121.3 1.1 multiply_convert_fusion
  122.5 0.9 slice.37
  123.4 3.2 %collective-permute-start.3 = (f32[2,512,128]{2,1,0:T(8,128)}, f32[2,512,128]{2,1,0:T(8,128)S(1)}, u32[]{:S(2)}, u32[]{:S(2)}) collective-permute-start(f32[2,512,128]{2,1,0:T(8,128)} %slice.37), channel_id=1, source_target_pairs={{0,1},{1,2},{2,3},{3,4},{4,5},{5,6},{6,7},{7,8},{8,9},{9,10},{10,1... | collective-permute-start | bytes 1572872 | tf_op jit(solution)/shard_map/ppermute | solution.py:23
  126.7 3.1 %collective-permute-start.5 = (f32[2,256,128]{2,1,0:T(8,128)S(1)}, f32[2,256,128]{2,1,0:T(8,128)S(1)}, u32[]{:S(2)}, u32[]{:S(2)}) collective-permute-start(f32[2,256,128]{2,1,0:T(8,128)S(1)} %slice.39), channel_id=1, source_target_pairs={{0,1},{1,2},{2,3},{3,4},{4,5},{5,6},{6,7},{7,8},{8,9},{9,10},{10,1... | collective-permute-start | bytes 786440 | tf_op jit(solution)/shard_map/ppermute | solution.py:23
  129.8 38.6 %project_slot.3 = (f32[2,6,768,128]{3,2,1,0:T(8,128)}, f32[3,256,256]{2,1,0:T(8,128)S(1)}) custom-call(s32[16,12]{1,0:T(8,128)S(1)} %bitcast.11, bf16[16,256,256]{2,1,0:T(8,128)(2,1)} %all-to-all-done.3.amp, f32[2,512,512]{2,1,0:T(8,128)} %obj.7, f32[2,512,256]{2,1,0:T(8,128)S(1)} %copy-done.9, f32[2,256,512]{2,1,0:T(8,128)} %collective-permute-done.1.below, ...), custom_call_target="tpu_custom_call" | custom-call | flops 8640000000 | bytes 40000000 | tf_op jit(solution)/shard_map/project_slot/pallas_call | solution.py:181
  168.5 40.5 %project_slot.4 = (f32[2,6,768,128]{3,2,1,0:T(8,128)}, f32[3,256,256]{2,1,0:T(8,128)S(1)}) custom-call(s32[16,12]{1,0:T(8,128)S(1)} %bitcast.12, bf16[16,256,256]{2,1,0:T(8,128)(2,1)} %all_to_all.26.amp, f32[2,512,512]{2,1,0:T(8,128)} %obj.7, f32[2,512,256]{2,1,0:T(8,128)} %copy-done.8, f32[2,256,512]{2,1,0:T(8,128)} %collective-permute-done.1.below, ...), custom_call_target="tpu_custom_call" | custom-call | flops 8640000000 | bytes 40000000 | tf_op jit(solution)/shard_map/project_slot/pallas_call | solution.py:181
  209.0 1.0 copy-done.5
  210.0 1.0 copy-done.7
  211.1 7.9 %project_slot.5 = (f32[2,6,768,128]{3,2,1,0:T(8,128)}, f32[3,256,256]{2,1,0:T(8,128)S(1)}) custom-call(s32[16,12]{1,0:T(8,128)S(1)} %bitcast.13, bf16[16,256,256]{2,1,0:T(8,128)(2,1)} %all-to-all-done.1.amp, f32[2,512,512]{2,1,0:T(8,128)} %obj.7, f32[2,512,256]{2,1,0:T(8,128)} %copy-done.8, f32[2,256,512]{2,1,0:T(8,128)} %collective-permute-done.1.below, ...), custom_call_target="tpu_custom_call" | custom-call | flops 8640000000 | bytes 40000000 | tf_op jit(solution)/shard_map/project_slot/pallas_call | solution.py:181
  219.0 77.4 %exchange.1 = (f32[2,512,512]{2,1,0:T(8,128)}, f32[2,256,256]{2,1,0:T(8,128)S(1)}) custom-call(f32[2,6,768,128]{3,2,1,0:T(8,128)} %get-tuple-element.16.acc, f32[3,256,256]{2,1,0:T(8,128)S(1)} %get-tuple-element.17.ps, f32[6,768,128]{2,1,0:T(8,128)} %copy-done, f32[2,512,128]{2,1,0:T(8,128)S(1)} %collective-permute-done.3.den_right, ...), custom_call_target="tpu_custom_call" | custom-call | tf_op jit(solution)/shard_map/exchange/pallas_call | solution.py:381
  296.3 3.1 %copy.14 = f32[2,512,512]{2,1,0:T(8,128)} copy(f32[2,512,512]{2,1,0:T(8,128)} %get-tuple-element.27) | data formatting | bytes 4194304
  299.4 0.8 copy.15
  (30 shorter events, 0.3 us)
Async XLA Ops:
  8.6 15.0 %all-to-all-start = ((s32[16,1,12]{2,1,0:T(1,128)}), s32[16,1,12]{2,1,0:T(1,128)S(1)}, u32[]{:S(2)}, u32[]{:S(2)}) async-start(s32[16,1,12]{2,1,0:T(1,128)} %bitcast.14), calls=%async_computation | async-start | bytes 16384 | tf_op jit(solution)/shard_map/all_to_all | solution.py:406
  55.0 4.9 %copy-start.10 = (f32[2,512,512]{2,1,0:T(8,128)S(1)}, f32[2,512,512]{2,1,0:T(8,128)}, u32[]{:S(2)}) copy-start(f32[2,512,512]{2,1,0:T(8,128)} %obj.7) | copy-start | bytes 6291460
  55.0 56.8 %all-to-all-start.3 = ((bf16[16,256,256]{2,1,0:T(8,128)(2,1)}), bf16[16,256,256]{2,1,0:T(8,128)(2,1)}, u32[]{:S(2)}, u32[]{:S(2)}) async-start(bf16[16,256,256]{2,1,0:T(8,128)(2,1)} %get-tuple-element.18), calls=%async_computation.3 | async-start | bytes 4194304 | tf_op jit(solution)/shard_map/all_to_all | solution.py:414
  60.0 7.7 %copy-start.1 = (f32[2,256,256]{2,1,0:T(8,128)S(1)}, f32[2,256,256]{2,1,0:T(8,128)}, u32[]{:S(2)}) copy-start(f32[2,256,256]{2,1,0:T(8,128)} %probe.7) | copy-start | bytes 1572868
  60.1 44.0 %collective-permute-start = (f32[2,512,256]{2,1,0:T(8,128)S(1)}, f32[2,512,256]{2,1,0:T(8,128)S(1)}, u32[]{:S(2)}, u32[]{:S(2)}) collective-permute-start(f32[2,512,256]{2,1,0:T(8,128)S(1)} %slice.28), channel_id=1, source_target_pairs={{1,0},{2,1},{3,2},{4,3},{5,4},{6,5},{7,6},{8,7},{9,8},{10,9},{11,1... | collective-permute-start | bytes 3145736 | tf_op jit(solution)/shard_map/ppermute | solution.py:23
  62.6 67.2 %collective-permute-start.1 = (f32[2,256,512]{2,1,0:T(8,128)}, f32[2,256,512]{2,1,0:T(8,128)}, u32[]{:S(2)}, u32[]{:S(2)}) collective-permute-start(f32[2,256,512]{2,1,0:T(8,128)} %slice.29), channel_id=1, source_target_pairs={{16,0},{32,16},{48,32},{64,48},{80,64},{96,80},{112,96},{17,1},{33... | collective-permute-start | bytes 3145736 | tf_op jit(solution)/shard_map/ppermute | solution.py:23
  73.5 49.0 %copy-start = (f32[6,768,128]{2,1,0:T(8,128)}, f32[6,768,128]{2,1,0:T(8,128)S(1)}, u32[]{:S(2)}) copy-start(f32[6,768,128]{2,1,0:T(8,128)S(1)} %denominator.1.den) | copy-start | bytes 7077892
  74.5 52.1 %collective-permute-start.4 = (f32[6,256,128]{2,1,0:T(8,128)}, f32[6,256,128]{2,1,0:T(8,128)S(1)}, u32[]{:S(2)}, u32[]{:S(2)}) collective-permute-start(f32[6,256,128]{2,1,0:T(8,128)} %slice.38), channel_id=1, source_target_pairs={{0,16},{16,32},{32,48},{48,64},{64,80},{80,96},{96,112},{1,17},{17... | collective-permute-start | bytes 2359304 | tf_op jit(solution)/shard_map/ppermute | solution.py:23
  104.9 1.0 copy-start.8
  105.9 23.9 %collective-permute-start.2 = (f32[2,256,256]{2,1,0:T(8,128)}, f32[2,256,256]{2,1,0:T(8,128)}, u32[]{:S(2)}, u32[]{:S(2)}) collective-permute-start(f32[2,256,256]{2,1,0:T(8,128)} %slice.36), channel_id=1, source_target_pairs={{16,0},{32,16},{48,32},{64,48},{80,64},{96,80},{112,96},{17,1},{33... | collective-permute-start | bytes 1572872 | tf_op jit(solution)/shard_map/ppermute | solution.py:23
  111.8 97.2 %all-to-all-start.1 = ((bf16[16,256,256]{2,1,0:T(8,128)(2,1)}), bf16[16,256,256]{2,1,0:T(8,128)(2,1)}, u32[]{:S(2)}, u32[]{:S(2)}) async-start(bf16[16,256,256]{2,1,0:T(8,128)(2,1)} %get-tuple-element.20), calls=%async_computation.1 | async-start | bytes 4194304 | tf_op jit(solution)/shard_map/all_to_all | solution.py:414
  120.2 9.6 %copy-start.2 = (f32[2,256,256]{2,1,0:T(8,128)S(1)}, f32[2,256,256]{2,1,0:T(8,128)}, u32[]{:S(2)}) copy-start(f32[2,256,256]{2,1,0:T(8,128)} %probe.7) | copy-start | bytes 1572868
  120.3 9.6 %copy-start.9 = (f32[2,512,256]{2,1,0:T(8,128)S(1)}, f32[2,512,256]{2,1,0:T(8,128)}, u32[]{:S(2)}) copy-start(f32[2,512,256]{2,1,0:T(8,128)} %copy-done.8) | copy-start | bytes 3145732
  122.5 46.0 %copy-start.4 = (bf16[512,512]{1,0:T(8,128)(2,1)}, bf16[512,512]{1,0:T(8,128)(2,1)S(1)}, u32[]{:S(2)}) copy-start(bf16[512,512]{1,0:T(8,128)(2,1)S(1)} %get-tuple-element.21.tb) | copy-start | bytes 1572868
  122.5 46.0 %copy-start.6 = (bf16[512,512]{1,0:T(8,128)(2,1)}, bf16[512,512]{1,0:T(8,128)(2,1)S(1)}, u32[]{:S(2)}) copy-start(bf16[512,512]{1,0:T(8,128)(2,1)S(1)} %get-tuple-element.22.ta) | copy-start | bytes 1572868
  123.4 95.5 %collective-permute-start.3 = (f32[2,512,128]{2,1,0:T(8,128)}, f32[2,512,128]{2,1,0:T(8,128)S(1)}, u32[]{:S(2)}, u32[]{:S(2)}) collective-permute-start(f32[2,512,128]{2,1,0:T(8,128)} %slice.37), channel_id=1, source_target_pairs={{0,1},{1,2},{2,3},{3,4},{4,5},{5,6},{6,7},{7,8},{8,9},{9,10},{10,1... | collective-permute-start | bytes 1572872 | tf_op jit(solution)/shard_map/ppermute | solution.py:23
  126.7 92.3 %collective-permute-start.5 = (f32[2,256,128]{2,1,0:T(8,128)S(1)}, f32[2,256,128]{2,1,0:T(8,128)S(1)}, u32[]{:S(2)}, u32[]{:S(2)}) collective-permute-start(f32[2,256,128]{2,1,0:T(8,128)S(1)} %slice.39), channel_id=1, source_target_pairs={{0,1},{1,2},{2,3},{3,4},{4,5},{5,6},{6,7},{7,8},{8,9},{9,10},{10,1... | collective-permute-start | bytes 786440 | tf_op jit(solution)/shard_map/ppermute | solution.py:23
  168.5 40.5 %copy-start.3 = (f32[2,256,256]{2,1,0:T(8,128)S(1)}, f32[2,256,256]{2,1,0:T(8,128)}, u32[]{:S(2)}) copy-start(f32[2,256,256]{2,1,0:T(8,128)} %probe.7) | copy-start | bytes 1572868
  209.0 1.0 copy-start.5
  210.0 1.0 copy-start.7

commit v2 on v1

v2 whole, which is shorter than its diff:
```python
import functools
import math

import jax
import jax.numpy as jnp
from jax import lax
from jax.experimental import pallas as pl
from jax.experimental.pallas import tpu as pltpu
from jax.sharding import PartitionSpec as P

W = 256
T = 512
SIDE = T + W
CAP = 3
PATS = 32
GROUP = 3
CH = 64
FRAME = W + 2 * CH
RB = 32
LB = 128
MIB = 2**20


def tables():
    steps = jnp.arange(W, dtype=jnp.int32)
    phase = steps[:, None] * steps[None, :] % W
    angles = phase.astype(jnp.float32) * (2.0 * math.pi / W)
    c = (jnp.cos(angles) / math.sqrt(W)).astype(jnp.bfloat16)
    s = (jnp.sin(angles) / math.sqrt(W)).astype(jnp.bfloat16)
    ta = jnp.concatenate([jnp.concatenate([c, s], 1), jnp.concatenate([-s, c], 1)], 0)
    tb = jnp.concatenate([jnp.concatenate([c, -s], 1), jnp.concatenate([s, c], 1)], 0)
    return ta, tb


def plan_kernel(meta, plan):
    ny, nx = lax.axis_size("ty"), lax.axis_size("tx")
    ty = lax.axis_index("ty")
    owner, row, col = meta[0:1, :], meta[1:2, :], meta[2:3, :]
    lane1 = lax.broadcasted_iota(jnp.int32, (1, LB), 1)
    rank = jnp.zeros((1, LB), jnp.int32)
    for d in range(1, PATS):
        rank = rank + jnp.where((pltpu.roll(owner, d, 1) == owner) & (lane1 >= d), 1, 0)
    target = jnp.where(lane1 < PATS, owner * 8 + rank, -1)
    row = jnp.minimum(row, ny * T - W - ty * T).astype(jnp.float32)
    col = jnp.minimum(col, nx * T - W - owner * T).astype(jnp.float32)
    one = jnp.ones((1, LB), jnp.float32)
    lane8 = lax.broadcasted_iota(jnp.int32, (8, LB), 1)
    sub8 = lax.broadcasted_iota(jnp.int32, (8, LB), 0)
    for o in range(nx):
        hit = (sub8 + 8 * o) == target
        tile = jnp.zeros((8, LB), jnp.float32)
        for f, field in enumerate((row, col, one, lane1.astype(jnp.float32))):
            value = jnp.sum(jnp.where(hit, field, 0.0), axis=1, keepdims=True)
            tile = jnp.where(lane8 == f, value, tile)
        plan[o] = tile.astype(jnp.int32)


def plan_of(owners, offsets):
    vm = pl.BlockSpec(memory_space=pltpu.VMEM)
    meta = jnp.pad(jnp.concatenate([owners, offsets], 1).T, ((0, 5), (0, LB - PATS)))
    return pl.pallas_call(
        plan_kernel,
        out_shape=jax.ShapeDtypeStruct((lax.axis_size("tx"), 8, LB), jnp.int32),
        in_specs=[vm],
        out_specs=vm,
        name="plan",
    )(meta)


def mesh_copy(src, dst, s, q, device):
    return pltpu.make_async_remote_copy(
        src_ref=src, dst_ref=dst, send_sem=s, recv_sem=q, device_id=device, device_id_type=pl.DeviceIdType.MESH
    )


def dot(a, b):
    return jnp.dot(a, b, preferred_element_type=jnp.float32)


def update_kernel(
    plan, amp, obj, probe, ta, tb, out, step,
    ext, sbuf, rbuf, ginfo, planm, infom, tpad, den, acc, ps, inv, win, xs, ys,
    d_right, d_below, d_corner, s_right, s_below, s_corner, g_right, g_below, g_corner, ra, sb, rb, gc, gd,
    si, qi, sp, qp, sh, qh, sc, qc, sd, qd, sa, qa, sbs, qb, scs, qcs, sds, qds, ses, qes, sl,
):
    ny, nx = lax.axis_size("ty"), lax.axis_size("tx")
    ty, tx = lax.axis_index("ty"), lax.axis_index("tx")
    down, up = lax.rem(ty + 1, ny), lax.rem(ty + ny - 1, ny)
    east, west = lax.rem(tx + 1, nx), lax.rem(tx + nx - 1, nx)
    barrier = pltpu.get_barrier_semaphore()
    greet = [(ty, lax.rem(tx + d, nx)) for d in range(1, nx)] + [(lax.rem(ty + d, ny), tx) for d in range(1, ny)]
    greet += [(up, west), (down, east)]
    for other in greet:
        pl.semaphore_signal(barrier, inc=1, device_id=other, device_id_type=pl.DeviceIdType.MESH)

    own = []
    for p in range(2):
        for b in range(4):
            own.append(pltpu.make_async_copy(obj.at[p, :, pl.ds(b * LB, LB)], ext.at[p, b, pl.ds(0, T), :], sl.at[len(own)]))
    for copy in own:
        copy.start()
    to_smem = pltpu.make_async_copy(plan, planm, sl.at[8])
    to_smem.start()

    def partner(i, sign):
        d = lax.rem(7 * i, nx)
        y, z = tx // 4, lax.rem(tx, 4)
        dy, dz = d // 4, lax.rem(d, 4)
        return lax.rem(y + nx + sign * dy, nx // 4) * 4 + lax.rem(z + 4 + sign * dz, 4)

    def info_copy(i):
        peer = partner(i, 1)
        return mesh_copy(plan.at[peer], ginfo.at[i], si.at[i - 1], qi.at[i - 1], (ty, peer))

    def amp_copy(m):
        return mesh_copy(sbuf.at[m], rbuf.at[m], sp.at[m], qp.at[m], (ty, partner(lax.rem(m, nx), 1)))

    halo, below = [], []
    for p in range(2):
        for b in range(2):
            k, lanes = len(halo), pl.ds(b * LB, LB)
            halo.append(mesh_copy(obj.at[p, :, lanes], ext.at[p, 4 + b, pl.ds(0, T), :], sh.at[k], qh.at[k], (ty, west)))
    for p in range(2):
        for b in range(4):
            k, lanes = 4 + len(below), pl.ds(b * LB, LB)
            below.append(mesh_copy(obj.at[p, pl.ds(0, W), lanes], ext.at[p, b, pl.ds(T, W), :], sh.at[k], qh.at[k], (up, tx)))

    pl.semaphore_wait(barrier, len(greet))
    lax.fori_loop(1, nx, lambda i, c: (info_copy(i).start(), c)[1], 0)
    for copy in halo + below:
        copy.start()
    ginfo[0] = plan[tx]
    to_smem.wait()

    def pack(m, carry):
        i, k = lax.rem(m, nx), m // nx

        @pl.when(i > 0)
        def _():
            sbuf[m] = amp[planm[partner(i, 1), k, 3]]
            amp_copy(m).start()

        @pl.when(i == 0)
        def _():
            rbuf[m] = amp[planm[tx, k, 3]]

        return carry

    lax.fori_loop(0, CAP * nx, pack, 0)

    for q in range(GROUP):
        for p in range(2):
            for b in range(5):
                tpad[q, p, b] = jnp.zeros((FRAME, LB), jnp.float32)

    def clear(i, carry):
        at = pl.ds(pl.multiple_of(i * CH, CH), CH)
        zero = jnp.zeros((CH, LB), jnp.float32)
        for b in range(SIDE // LB):
            den[b, at, :] = zero
            for p in range(2):
                acc[p, b, at, :] = zero
        return carry

    lax.fori_loop(0, SIDE // CH, clear, 0)
    ps[...] = jnp.zeros(ps.shape, jnp.float32)
    lax.fori_loop(1, nx, lambda i, c: (info_copy(i).wait_recv(), c)[1], 0)
    to_smem = pltpu.make_async_copy(ginfo, infom, sl.at[8])
    to_smem.start()
    to_smem.wait()
    lane = lax.broadcasted_iota(jnp.int32, (RB, LB), 1)

    def windows(g):
        found = []
        for q in range(GROUP):
            m = g * GROUP + q
            i, k = lax.rem(m, nx), m // nx
            found.append((infom[i, k, 0], infom[i, k, 1], infom[i, k, 2].astype(jnp.float32)))
        return found

    def place(q, p, k, halves, cs):
        high = lane >= cs
        a = [pltpu.roll(half, cs, 1) for half in halves]
        at = slice(CH + k, CH + k + RB)
        tpad[q, p, 1, at, :] = jnp.where(high, a[0], 0.0)
        tpad[q, p, 2, at, :] = jnp.where(high, a[1], a[0])
        tpad[q, p, 3, at, :] = jnp.where(high, 0.0, a[1])

    def pull(found, planes):
        cols = [[jnp.clip(b - c // LB, -1, 3) + 1 for b in range(SIDE // LB)] for _, c, _ in found]

        def rows(j, carry):
            y0 = pl.multiple_of(j * CH, CH)
            starts = [jnp.clip(y0 - r, -CH, W) + CH for r, _, _ in found]
            for b in range(SIDE // LB):
                for p, ref in enumerate(planes):
                    v = ref[b, pl.ds(y0, CH), :]
                    for q in range(GROUP):
                        v = v + tpad[q, p, cols[q][b], pl.ds(starts[q], CH), :]
                    ref[b, pl.ds(y0, CH), :] = v
            return carry

        lax.fori_loop(0, SIDE // CH, rows, 0)

    def spread(g, carry):
        found = windows(g)
        for k in range(0, W, RB):
            power = []
            for h in range(2):
                at = slice(h * LB, h * LB + LB)
                pr, pi = probe[0, k:k + RB, at], probe[1, k:k + RB, at]
                power.append(pr * pr + pi * pi)
            for q in range(GROUP):
                place(q, 0, k, [x * found[q][2] for x in power], lax.rem(found[q][1], LB))
        pull(found, [den])
        return carry

    groups = CAP * nx // GROUP
    lax.fori_loop(0, groups, spread, 0)
    d_strips = [
        mesh_copy(den.at[pl.ds(4, 2), pl.ds(0, T), :], d_right, sd.at[0], qd.at[0], (ty, east)),
        mesh_copy(den.at[pl.ds(4, 2), pl.ds(T, W), :], d_corner, sd.at[1], qd.at[1], (down, east)),
        mesh_copy(den.at[pl.ds(0, 4), pl.ds(T, W), :], d_below, sd.at[2], qd.at[2], (down, tx)),
    ]
    for copy in d_strips:
        copy.start()

    for copy in halo:
        copy.wait_recv()
    corner = []
    for p in range(2):
        strip = ext.at[p, pl.ds(4, 2), pl.ds(0, W), :]
        corner.append(mesh_copy(strip, ext.at[p, pl.ds(4, 2), pl.ds(T, W), :], sc.at[p], qc.at[p], (up, tx)))
    for copy in corner:
        copy.start()
    for copy in own:
        copy.wait()
    for copy in below + corner:
        copy.wait_recv()

    def half(t, q):
        y = dot(t[...], xs[q]).astype(jnp.bfloat16)
        ys[q, :, :W] = y[:W]
        ys[q, :, W:] = y[W:]

    def group(g, carry):
        found = windows(g)
        for q in range(GROUP):
            m = g * GROUP + q

            @pl.when(lax.rem(m, nx) > 0)
            def _():
                amp_copy(m).wait_recv()

        for q in range(GROUP):
            r, c, _ = found[q]
            cb, cs = c // LB, lax.rem(c, LB)
            back = lax.rem(LB - cs, LB)
            low = lane < LB - cs
            for k in range(0, W, RB):
                o = []
                for p in range(2):
                    b = [pltpu.roll(ext[p, cb + j, pl.ds(r + k, RB), :], back, 1) for j in range(3)]
                    o.append([jnp.where(low, b[0], b[1]), jnp.where(low, b[1], b[2])])
                for h in range(2):
                    at = slice(h * LB, h * LB + LB)
                    ore, oim = o[0][h], o[1][h]
                    win[q, 0, k:k + RB, at] = ore
                    win[q, 1, k:k + RB, at] = oim
                    pr, pi = probe[0, k:k + RB, at], probe[1, k:k + RB, at]
                    xs[q, k:k + RB, at] = (pr * ore - pi * oim).astype(jnp.bfloat16)
                    xs[q, W + k:W + k + RB, at] = (pr * oim + pi * ore).astype(jnp.bfloat16)
        for q in range(GROUP):
            half(ta, q)
        for q in range(GROUP):
            z = dot(ys[q], tb[...])
            zr, zi = z[:, :W], z[:, W:]
            f = rbuf[g * GROUP + q].astype(jnp.float32) * lax.rsqrt(zr * zr + zi * zi + 0.01)
            xs[q, :W] = (zr * f).astype(jnp.bfloat16)
            xs[q, W:] = (zi * f).astype(jnp.bfloat16)
        for q in range(GROUP):
            half(tb, q)
        zs = [dot(ys[q], ta[...]) for q in range(GROUP)]
        for k in range(0, W, RB):
            terms = [[[], []] for q in range(GROUP)]
            for h in range(2):
                at = slice(h * LB, h * LB + LB)
                pr, pi = probe[0, k:k + RB, at], probe[1, k:k + RB, at]
                sums = None
                for q in range(GROUP):
                    live = found[q][2]
                    ore, oim = win[q, 0, k:k + RB, at], win[q, 1, k:k + RB, at]
                    dr = (zs[q][k:k + RB, at] - (pr * ore - pi * oim)) * live
                    di = (zs[q][k:k + RB, W + h * LB:W + h * LB + LB] - (pr * oim + pi * ore)) * live
                    terms[q][0].append(pr * dr + pi * di)
                    terms[q][1].append(pr * di - pi * dr)
                    mine = (ore * dr + oim * di, ore * di - oim * dr, (ore * ore + oim * oim) * live)
                    sums = mine if sums is None else tuple(x + y for x, y in zip(sums, mine))
                for j in range(3):
                    ps[j, k:k + RB, at] += sums[j]
            for q in range(GROUP):
                for p in range(2):
                    place(q, p, k, terms[q][p], lax.rem(found[q][1], LB))
        pull(found, [acc.at[0], acc.at[1]])
        return carry

    lax.fori_loop(0, groups, group, 0)

    def send(*args):
        copy = mesh_copy(*args)
        copy.start()
        return copy

    rows = W // ny
    stage_a = []
    for d in range(1, ny):
        peer = lax.rem(ty + d, ny)
        piece = ps.at[:, pl.ds(pl.multiple_of(peer * rows, rows), rows), :]
        stage_a.append(send(piece, ra.at[ty], sa.at[d - 1], qa.at[d - 1], (peer, tx)))
    for p in range(2):
        for b in range(2):
            s_right[p, b] = acc[p, 4 + b, :T, :].astype(jnp.bfloat16)
    strips = [send(s_right, g_right, ses.at[0], qes.at[0], (ty, east))]
    for p in range(2):
        for b in range(2):
            s_corner[p, b] = acc[p, 4 + b, T:, :].astype(jnp.bfloat16)
    strips.append(send(s_corner, g_corner, ses.at[1], qes.at[1], (down, east)))
    for p in range(2):
        for b in range(4):
            s_below[p, b] = acc[p, b, T:, :].astype(jnp.bfloat16)
    strips.append(send(s_below, g_below, ses.at[2], qes.at[2], (down, tx)))
    ra[ty] = ps[:, pl.ds(pl.multiple_of(ty * rows, rows), rows), :]

    for copy in d_strips:
        copy.wait_recv()
    has_west = jnp.where(tx > 0, 1.0, 0.0)
    has_north = jnp.where(ty > 0, 1.0, 0.0)
    has_both = has_west * has_north
    for b in range(4):
        top, rest = den[b, :W, :] + has_north * d_below[b], den[b, W:T, :]
        if b < 2:
            top = top + (has_west * d_right[b, :W, :] + has_both * d_corner[b])
            rest = rest + has_west * d_right[b, W:, :]
        inv[b, :W, :] = 1.0 / (top + 1.0)
        inv[b, W:, :] = 1.0 / (rest + 1.0)

    for copy in stage_a:
        copy.wait_recv()
    total = ra[0]
    for j in range(1, ny):
        total = total + ra[j]
    for j in range(nx):
        p, g, h = j // (nx // 2), j // 2 % (rows // 8), j % 2
        lanes = slice(h * LB, h * LB + LB)
        sb[j, 0] = total[p, g * 8:g * 8 + 8, lanes]
        sb[j, 1] = total[2, g * 8:g * 8 + 8, lanes]
    stage_b = []
    for d in range(1, nx):
        peer = lax.rem(tx + d, nx)
        stage_b.append(send(sb.at[peer], rb.at[tx], sbs.at[d - 1], qb.at[d - 1], (ty, peer)))
    rb[tx] = sb[tx]
    for copy in stage_b:
        copy.wait_recv()
    total = rb[0]
    for j in range(1, nx):
        total = total + rb[j]
    gc[tx] = total[0] / jnp.sqrt(total[1] + 1.0)
    stage_c = []
    for d in range(1, nx):
        peer = lax.rem(tx + d, nx)
        stage_c.append(send(gc.at[tx], gc.at[tx], scs.at[d - 1], qcs.at[d - 1], (ty, peer)))
    for copy in stage_c:
        copy.wait_recv()
    gd[ty] = gc[...]
    stage_d = []
    for d in range(1, ny):
        peer = lax.rem(ty + d, ny)
        stage_d.append(send(gc, gd.at[ty], sds.at[d - 1], qds.at[d - 1], (peer, tx)))

    for copy in strips:
        copy.wait_recv()

    def upper(i, carry):
        at = pl.ds(pl.multiple_of(i * RB, RB), RB)
        for b in range(4):
            lanes = slice(b * LB, b * LB + LB)
            for p in range(2):
                num = acc[p, b, at, :] + has_north * g_below[p, b, at, :].astype(jnp.float32)
                if b < 2:
                    num = num + has_west * g_right[p, b, at, :].astype(jnp.float32)
                    num = num + has_both * g_corner[p, b, at, :].astype(jnp.float32)
                out[p, at, lanes] = ext[p, b, at, :] + num * inv[b, at, :]
        return carry

    def lower(i, carry):
        at = pl.ds(pl.multiple_of(i * RB, RB), RB)
        for b in range(4):
            lanes = slice(b * LB, b * LB + LB)
            for p in range(2):
                num = acc[p, b, at, :]
                if b < 2:
                    num = num + has_west * g_right[p, b, at, :].astype(jnp.float32)
                out[p, at, lanes] = ext[p, b, at, :] + num * inv[b, at, :]
        return carry

    lax.fori_loop(0, W // RB, upper, 0)
    lax.fori_loop(W // RB, T // RB, lower, 0)

    for copy in stage_d:
        copy.wait_recv()
    for t in range(ny):
        for j in range(nx):
            p, g, h = j // (nx // 2), j // 2 % (rows // 8), j % 2
            step[p, t * rows + g * 8:t * rows + g * 8 + 8, h * LB:h * LB + LB] = gd[t, j]
    for copy in halo + below + corner + d_strips + stage_a + strips + stage_b + stage_c + stage_d:
        copy.wait_send()
    lax.fori_loop(1, nx, lambda i, c: (info_copy(i).wait_send(), c)[1], 0)

    def sent(m, carry):
        @pl.when(lax.rem(m, nx) > 0)
        def _():
            amp_copy(m).wait_send()

        return carry

    lax.fori_loop(0, CAP * nx, sent, 0)


def update(plan, amp, obj, probe, ta, tb):
    ny, nx = lax.axis_size("ty"), lax.axis_size("tx")
    vm = pl.BlockSpec(memory_space=pltpu.VMEM)
    bf, f32, i32 = jnp.bfloat16, jnp.float32, jnp.int32
    dma = pltpu.SemaphoreType.DMA
    blocks = SIDE // LB
    strips = [(2, 2, T, LB), (2, 4, W, LB), (2, 2, W, LB)]
    sems = [nx - 1, nx - 1, CAP * nx, CAP * nx, 12, 12, 2, 2, 3, 3]
    sems += [ny - 1, ny - 1, nx - 1, nx - 1, nx - 1, nx - 1, ny - 1, ny - 1, 3, 3, 9]
    return pl.pallas_call(
        update_kernel,
        out_shape=(jax.ShapeDtypeStruct(obj.shape, f32), jax.ShapeDtypeStruct((2, W, W), f32)),
        in_specs=[vm, vm, pl.BlockSpec(memory_space=pl.ANY), vm, vm, vm],
        out_specs=(vm, vm),
        scratch_shapes=[
            pltpu.VMEM((2, blocks, SIDE, LB), f32),
            pltpu.VMEM((CAP * nx, W, W), bf),
            pltpu.VMEM((CAP * nx, W, W), bf),
            pltpu.VMEM((nx, 8, LB), i32),
            pltpu.SMEM((nx, 8, LB), i32),
            pltpu.SMEM((nx, 8, LB), i32),
            pltpu.VMEM((GROUP, 2, 5, FRAME, LB), f32),
            pltpu.VMEM((blocks, SIDE, LB), f32),
            pltpu.VMEM((2, blocks, SIDE, LB), f32),
            pltpu.VMEM((3, W, W), f32),
            pltpu.VMEM((4, T, LB), f32),
            pltpu.VMEM((GROUP, 2, W, W), f32),
            pltpu.VMEM((GROUP, 2 * W, W), bf),
            pltpu.VMEM((GROUP, W, 2 * W), bf),
        ]
        + [pltpu.VMEM(x[1:], f32) for x in strips]
        + [pltpu.VMEM(x, bf) for x in strips + strips]
        + [
            pltpu.VMEM((ny, 3, W // ny, W), f32),
            pltpu.VMEM((nx, 2, 8, LB), f32),
            pltpu.VMEM((nx, 2, 8, LB), f32),
            pltpu.VMEM((nx, 8, LB), f32),
            pltpu.VMEM((ny, nx, 8, LB), f32),
        ]
        + [dma((k,)) for k in sems],
        compiler_params=pltpu.CompilerParams(vmem_limit_bytes=60 * MIB, collective_id=0, has_side_effects=True),
        name="update",
    )(plan, amp, obj, probe, ta, tb)


def local(amplitudes, owners, offsets, object_field, probe):
    plan = plan_of(owners, offsets)
    ta, tb = tables()
    return update(plan, amplitudes, object_field, probe, ta, tb)


def solution(mesh):
    return jax.shard_map(
        local,
        mesh=mesh,
        in_specs=(
            P(("ty", "tx"), None, None),
            P(("ty", "tx"), None),
            P(("ty", "tx"), None),
            P(None, "ty", "tx"),
            P(),
        ),
        out_specs=(P(None, "ty", "tx"), P()),
        check_vma=False,
    )
```

time: 301 us -> 210 us (0.70)
  starting transfers between devices: 43.7 us -> 0 us
  blocking collectives: 31.4 us -> 0 us
  waiting for transfers between devices: 27.5 us -> 0 us
  Pallas kernels: 175 us -> 201 us
  local copies, waits for them, and re-layouts: 19.1 us -> 4.53 us
    all_to_all x1 -> x0, blocking collectives: 31.4 us -> none  [local(): lax.all_to_all(packed[slot], 'tx', split_axis=0, concat_axis=0, tiled=True)]
    ppermute x6 -> x0, waiting for transfers between devices: 26.6 us -> none  [shifted(): lax.ppermute(value, axis, [(source, source + steps) for source in range(i...]
    pallas_call x6 -> x2, Pallas kernels: 175 us -> 201 us  [the longest x1 199 us: update(): pl.pallas_call(update_kernel, out_shape=(jax.ShapeDtypeStruct(obj.shape,...]
    all_to_all x3 -> x0, starting transfers between devices: 22 us -> none  [the longest x2 13.4 us: local(): lax.all_to_all(packed[slot], 'tx', split_axis=0, concat_axis=0, tiled=True)]
    ppermute x6 -> x0, starting transfers between devices: 21.7 us -> none  [shifted(): lax.ppermute(value, axis, [(source, source + steps) for source in range(i...]
    unnamed x26 -> x4, local copies, waits for them, and re-layouts: 9.67 us -> 3.93 us
    squeeze x1 -> x0, local copies, waits for them, and re-layouts: 5.53 us -> none  [local(): packed[slot]]
    slice x6 -> x0, local copies, waits for them, and re-layouts: 3.93 us -> none  [the longest x1 1.05 us: local(): below = shifted(object_field[:, :W, :], 'ty', -1)]
  transfers between devices with their start and end apart: 9 -> 0, of which waited for: 2 -> 0; matrix products, arithmetic and copies ran while one was open for 4% -> 0% of each run, Pallas kernels for 31% -> 0%
where the time goes in v2:
time: 210 us
  Pallas kernels  201 us (96%)
  local copies, waits for them, and re-layouts  4.53 us (2%)
  other arithmetic  3.83 us (2%)
    pallas_call x1, Pallas kernels, update(): pl.pallas_call(update_kernel, out_shape=(jax.ShapeDtypeStruct(obj.shape,...  199 us

profile of v2, /device:TPU:1, one launch (start us, length us, event | category | flops | bytes accessed | tf_op | source)
XLA Modules:
  0.0 209.7 jit_solution(14853001882875318703)
XLA Ops:
  0.6 0.7 add_bitcast_fusion
  1.3 0.6 pad.4.meta
  1.9 1.6 plan.1
  3.5 1.0 fusion.8
  4.5 1.1 multiply_convert_fusion
  5.6 1.0 fusion.1
  6.6 199.1 %update.1 = (f32[2,512,512]{2,1,0:T(8,128)}, f32[2,256,256]{2,1,0:T(8,128)}) custom-call(s32[16,8,128]{2,1,0:T(8,128)} %plan.1, bf16[32,256,256]{2,1,0:T(8,128)(2,1)} %amp.1, f32[2,512,512]{2,1,0:T(8,128)} %obj.1, f32[2,256,256]{2,1,0:T(8,128)} %probe.1, bf16[512,512]{1,0:T(8,128)(2,1)} %get-tuple-element.3.ta, bf16[512,512]{1,0:T(8,128)(2,1)} %get-tuple-element.2.tb), custom_call_target="tpu_custom_call" | custom-call | tf_op jit(solution)/shard_map/update/pallas_call | solution.py:438
  205.8 0.0 copy-start
  205.8 3.1 %copy.9 = f32[2,512,512]{2,1,0:T(8,128)} copy(f32[2,512,512]{2,1,0:T(8,128)} %get-tuple-element.8) | data formatting | bytes 4194304
  208.9 0.0 copy-done
  208.9 0.8 copy.10
Async XLA Ops:
  205.8 3.1 %copy-start = (f32[2,256,256]{2,1,0:T(8,128)S(1)}, f32[2,256,256]{2,1,0:T(8,128)}, u32[]{:S(2)}) copy-start(f32[2,256,256]{2,1,0:T(8,128)} %get-tuple-element.9) | copy-start | bytes 1572868

commit v3 on v2

--- a/solution.py
+++ b/solution.py
@@ -3,6 +3,8 @@
 
 import jax
 import jax.numpy as jnp
+import ml_dtypes
+import numpy as np
 from jax import lax
 from jax.experimental import pallas as pl
 from jax.experimental.pallas import tpu as pltpu
@@ -14,6 +16,8 @@
 CAP = 3
 PATS = 32
 GROUP = 3
+FIRST = 16
+AHEAD = 3
 CH = 64
 FRAME = W + 2 * CH
 RB = 32
@@ -22,14 +26,12 @@
 
 
 def tables():
-    steps = jnp.arange(W, dtype=jnp.int32)
-    phase = steps[:, None] * steps[None, :] % W
-    angles = phase.astype(jnp.float32) * (2.0 * math.pi / W)
-    c = (jnp.cos(angles) / math.sqrt(W)).astype(jnp.bfloat16)
-    s = (jnp.sin(angles) / math.sqrt(W)).astype(jnp.bfloat16)
-    ta = jnp.concatenate([jnp.concatenate([c, s], 1), jnp.concatenate([-s, c], 1)], 0)
-    tb = jnp.concatenate([jnp.concatenate([c, -s], 1), jnp.concatenate([s, c], 1)], 0)
-    return ta, tb
+    steps = np.arange(W)
+    phase = (steps[:, None] * steps[None, :] % W).astype(np.float32)
+    angles = phase * np.float32(2.0 * math.pi / W)
+    c, s = np.cos(angles) / np.float32(math.sqrt(W)), np.sin(angles) / np.float32(math.sqrt(W))
+    ta, tb = np.block([[c, s], [-s, c]]), np.block([[c, -s], [s, c]])
+    return jnp.asarray(ta.astype(ml_dtypes.bfloat16)), jnp.asarray(tb.astype(ml_dtypes.bfloat16))
 
 
 def plan_kernel(meta, plan):
@@ -115,20 +117,30 @@
     def amp_copy(m):
         return mesh_copy(sbuf.at[m], rbuf.at[m], sp.at[m], qp.at[m], (ty, partner(lax.rem(m, nx), 1)))
 
-    halo, below = [], []
+    below = []
+    for p in range(2):
+        for b in range(4):
+            k, lanes = len(below), pl.ds(b * LB, LB)
+            below.append(mesh_copy(obj.at[p, pl.ds(0, W), lanes], ext.at[p, b, pl.ds(T, W), :], sh.at[k], qh.at[k], (up, tx)))
+
+    halo = []
+    for r in range(2):
+        for p in range(2):
+            for b in range(2):
+                k, at = len(halo), pl.ds(r * W, W)
+                part = obj.at[p, at, pl.ds(b * LB, LB)]
+                halo.append(mesh_copy(part, ext.at[p, 4 + b, at, :], sc.at[k], qc.at[k], (ty, west)))
+    corner = []
     for p in range(2):
         for b in range(2):
-            k, lanes = len(halo), pl.ds(b * LB, LB)
-            halo.append(mesh_copy(obj.at[p, :, lanes], ext.at[p, 4 + b, pl.ds(0, T), :], sh.at[k], qh.at[k], (ty, west)))
-    for p in range(2):
-        for b in range(4):
-            k, lanes = 4 + len(below), pl.ds(b * LB, LB)
-            below.append(mesh_copy(obj.at[p, pl.ds(0, W), lanes], ext.at[p, b, pl.ds(T, W), :], sh.at[k], qh.at[k], (up, tx)))
+            k, part = 8 + len(corner), ext.at[p, 4 + b, pl.ds(0, W), :]
+            corner.append(mesh_copy(part, ext.at[p, 4 + b, pl.ds(T, W), :], sc.at[k], qc.at[k], (up, tx)))
 
     pl.semaphore_wait(barrier, len(greet))
     lax.fori_loop(1, nx, lambda i, c: (info_copy(i).start(), c)[1], 0)
-    for copy in halo + below:
-        copy.start()
+    for pair in zip(halo, below):
+        for copy in pair:
+            copy.start()
     ginfo[0] = plan[tx]
     to_smem.wait()
 
@@ -146,7 +158,7 @@
 
         return carry
 
-    lax.fori_loop(0, CAP * nx, pack, 0)
+    lax.fori_loop(0, FIRST, pack, 0)
 
     for q in range(GROUP):
         for p in range(2):
@@ -225,17 +237,12 @@
     for copy in d_strips:
         copy.start()
 
-    for copy in halo:
-        copy.wait_recv()
-    corner = []
-    for p in range(2):
-        strip = ext.at[p, pl.ds(4, 2), pl.ds(0, W), :]
-        corner.append(mesh_copy(strip, ext.at[p, pl.ds(4, 2), pl.ds(T, W), :], sc.at[p], qc.at[p], (up, tx)))
-    for copy in corner:
-        copy.start()
+    for arrived, onward in zip(halo[:4], corner):
+        arrived.wait_recv()
+        onward.start()
     for copy in own:
         copy.wait()
-    for copy in below + corner:
+    for copy in halo[4:] + below + corner:
         copy.wait_recv()
 
     def half(t, q):
@@ -245,6 +252,13 @@
 
     def group(g, carry):
         found = windows(g)
+        for q in range(AHEAD):
+            later = FIRST + g * AHEAD + q
+
+            @pl.when(later < CAP * nx)
+            def _():
+                pack(later, 0)
+
         for q in range(GROUP):
             m = g * GROUP + q
 
@@ -317,18 +331,22 @@
         peer = lax.rem(ty + d, ny)
         piece = ps.at[:, pl.ds(pl.multiple_of(peer * rows, rows), rows), :]
         stage_a.append(send(piece, ra.at[ty], sa.at[d - 1], qa.at[d - 1], (peer, tx)))
-    for p in range(2):
-        for b in range(2):
+    strips = []
+
+    def strip(kind, p, b):
+        k = len(strips)
+        if kind == 0:
             s_right[p, b] = acc[p, 4 + b, :T, :].astype(jnp.bfloat16)
-    strips = [send(s_right, g_right, ses.at[0], qes.at[0], (ty, east))]
-    for p in range(2):
-        for b in range(2):
+            strips.append(send(s_right.at[p, b], g_right.at[p, b], ses.at[k], qes.at[k], (ty, east)))
+        elif kind == 1:
             s_corner[p, b] = acc[p, 4 + b, T:, :].astype(jnp.bfloat16)
-    strips.append(send(s_corner, g_corner, ses.at[1], qes.at[1], (down, east)))
-    for p in range(2):
-        for b in range(4):
+            strips.append(send(s_corner.at[p, b], g_corner.at[p, b], ses.at[k], qes.at[k], (down, east)))
+        else:
             s_below[p, b] = acc[p, b, T:, :].astype(jnp.bfloat16)
-    strips.append(send(s_below, g_below, ses.at[2], qes.at[2], (down, tx)))
+            strips.append(send(s_below.at[p, b], g_below.at[p, b], ses.at[k], qes.at[k], (down, tx)))
+
+    for what in ((0, 0, 0), (2, 0, 0), (0, 0, 1), (2, 0, 1), (0, 1, 0), (2, 0, 2)):
+        strip(*what)
     ra[ty] = ps[:, pl.ds(pl.multiple_of(ty * rows, rows), rows), :]
 
     for copy in d_strips:
@@ -359,6 +377,8 @@
         peer = lax.rem(tx + d, nx)
         stage_b.append(send(sb.at[peer], rb.at[tx], sbs.at[d - 1], qb.at[d - 1], (ty, peer)))
     rb[tx] = sb[tx]
+    for what in ((0, 1, 1), (2, 0, 3), (1, 0, 0)):
+        strip(*what)
     for copy in stage_b:
         copy.wait_recv()
     total = rb[0]
@@ -369,6 +389,8 @@
     for d in range(1, nx):
         peer = lax.rem(tx + d, nx)
         stage_c.append(send(gc.at[tx], gc.at[tx], scs.at[d - 1], qcs.at[d - 1], (ty, peer)))
+    for what in ((1, 0, 1), (2, 1, 0), (1, 1, 0), (2, 1, 1), (1, 1, 1)):
+        strip(*what)
     for copy in stage_c:
         copy.wait_recv()
     gd[ty] = gc[...]
@@ -377,6 +399,8 @@
         peer = lax.rem(ty + d, ny)
         stage_d.append(send(gc, gd.at[ty], sds.at[d - 1], qds.at[d - 1], (peer, tx)))
 
+    for what in ((2, 1, 2), (2, 1, 3)):
+        strip(*what)
     for copy in strips:
         copy.wait_recv()
 
@@ -433,8 +457,8 @@
     dma = pltpu.SemaphoreType.DMA
     blocks = SIDE // LB
     strips = [(2, 2, T, LB), (2, 4, W, LB), (2, 2, W, LB)]
-    sems = [nx - 1, nx - 1, CAP * nx, CAP * nx, 12, 12, 2, 2, 3, 3]
-    sems += [ny - 1, ny - 1, nx - 1, nx - 1, nx - 1, nx - 1, ny - 1, ny - 1, 3, 3, 9]
+    sems = [nx - 1, nx - 1, CAP * nx, CAP * nx, 8, 8, 12, 12, 3, 3]
+    sems += [ny - 1, ny - 1, nx - 1, nx - 1, nx - 1, nx - 1, ny - 1, ny - 1, 16, 16, 9]
     return pl.pallas_call(
         update_kernel,
         out_shape=(jax.ShapeDtypeStruct(obj.shape, f32), jax.ShapeDtypeStruct((2, W, W), f32)),

time: 210 us -> 181 us (0.86)
  Pallas kernels: 201 us -> 175 us
  other arithmetic: 3.83 us -> 0.69 us
    pallas_call x1, Pallas kernels: 199 us -> 174 us  [update(): pl.pallas_call(update_kernel, out_shape=(jax.ShapeDtypeStruct(obj.shape,...]
where the time goes in v3:
time: 181 us
  Pallas kernels  175 us (97%)
  local copies, waits for them, and re-layouts  4.53 us (3%)
    pallas_call x1, Pallas kernels, update(): pl.pallas_call(update_kernel, out_shape=(jax.ShapeDtypeStruct(obj.shape,...  174 us
    unnamed x4, local copies, waits for them, and re-layouts  3.93 us

profile of v3, /device:TPU:1, one launch (start us, length us, event | category | flops | bytes accessed | tf_op | source)
XLA Modules:
  0.0 181.1 jit_solution(7054820365695460742)
XLA Ops:
  0.6 0.7 add_bitcast_fusion
  1.3 0.6 pad.4.meta
  1.9 1.6 plan.1
  3.5 173.7 %update.1 = (f32[2,512,512]{2,1,0:T(8,128)}, f32[2,256,256]{2,1,0:T(8,128)}) custom-call(s32[16,8,128]{2,1,0:T(8,128)} %plan.1, bf16[32,256,256]{2,1,0:T(8,128)(2,1)} %amp.1, f32[2,512,512]{2,1,0:T(8,128)} %obj.1, f32[2,256,256]{2,1,0:T(8,128)} %probe.1, bf16[512,512]{1,0:T(8,128)(2,1)} %constant.6.clone.ta, bf16[512,512]{1,0:T(8,128)(2,1)} %constant.7.clone.tb), custom_call_target="tpu_custom_call" | custom-call | tf_op jit(solution)/shard_map/update/pallas_call | solution.py:462
  177.1 0.0 copy-start
  177.2 3.1 %copy.11 = f32[2,512,512]{2,1,0:T(8,128)} copy(f32[2,512,512]{2,1,0:T(8,128)} %get-tuple-element.4) | data formatting | bytes 4194304
  180.3 0.0 copy-done
  180.3 0.8 copy.12
Async XLA Ops:
  177.1 3.1 %copy-start = (f32[2,256,256]{2,1,0:T(8,128)S(1)}, f32[2,256,256]{2,1,0:T(8,128)}, u32[]{:S(2)}) copy-start(f32[2,256,256]{2,1,0:T(8,128)} %get-tuple-element.5) | copy-start | bytes 1572868

commit v4 on v3

--- a/solution.py
+++ b/solution.py
@@ -16,7 +16,7 @@
 CAP = 3
 PATS = 32
 GROUP = 3
-FIRST = 16
+FIRST = 12
 AHEAD = 3
 CH = 64
 FRAME = W + 2 * CH
@@ -105,7 +105,7 @@
     to_smem.start()
 
     def partner(i, sign):
-        d = lax.rem(7 * i, nx)
+        d = lax.rem(9 * i, nx)
         y, z = tx // 4, lax.rem(tx, 4)
         dy, dz = d // 4, lax.rem(d, 4)
         return lax.rem(y + nx + sign * dy, nx // 4) * 4 + lax.rem(z + 4 + sign * dz, 4)

time: 181 us -> 180 us (level)
  no operation moved by 1% of the time
where the time goes in v4:
time: 180 us; the launch traced here: 181 us
  Pallas kernels  175 us (97%)
  local copies, waits for them, and re-layouts  4.53 us (3%)
    pallas_call x1, Pallas kernels, update(): pl.pallas_call(update_kernel, out_shape=(jax.ShapeDtypeStruct(obj.shape,...  173 us
    unnamed x4, local copies, waits for them, and re-layouts  3.93 us

profile of v4, /device:TPU:1, one launch (start us, length us, event | category | flops | bytes accessed | tf_op | source)
XLA Modules:
  0.0 180.9 jit_solution(5516540010866001651)
XLA Ops:
  0.6 0.7 add_bitcast_fusion
  1.3 0.6 pad.4.meta
  1.9 1.6 plan.1
  3.5 173.4 %update.1 = (f32[2,512,512]{2,1,0:T(8,128)}, f32[2,256,256]{2,1,0:T(8,128)}) custom-call(s32[16,8,128]{2,1,0:T(8,128)} %plan.1, bf16[32,256,256]{2,1,0:T(8,128)(2,1)} %amp.1, f32[2,512,512]{2,1,0:T(8,128)} %obj.1, f32[2,256,256]{2,1,0:T(8,128)} %probe.1, bf16[512,512]{1,0:T(8,128)(2,1)} %constant.6.clone.ta, bf16[512,512]{1,0:T(8,128)(2,1)} %constant.7.clone.tb), custom_call_target="tpu_custom_call" | custom-call | tf_op jit(solution)/shard_map/update/pallas_call | solution.py:462
  176.9 0.0 copy-start
  176.9 3.1 %copy.11 = f32[2,512,512]{2,1,0:T(8,128)} copy(f32[2,512,512]{2,1,0:T(8,128)} %get-tuple-element.4) | data formatting | bytes 4194304
  180.1 0.0 copy-done
  180.1 0.8 copy.12
Async XLA Ops:
  176.9 3.1 %copy-start = (f32[2,256,256]{2,1,0:T(8,128)S(1)}, f32[2,256,256]{2,1,0:T(8,128)}, u32[]{:S(2)}) copy-start(f32[2,256,256]{2,1,0:T(8,128)} %get-tuple-element.5) | copy-start | bytes 1572868
